TPU v7x, 32 devices: a whole 2x2x4 slice. The times are simulated.
32 devices in a mesh: grp: 2 (over x), dp: 16 (over z, y, core).
Axes of the slice: x: 2, y: 2, z: 4, core: 2. Of those that a mesh axis runs over, the one named last changes fastest.
Arguments:
- teacher_in: bfloat16 [8192, 1664], P('dp'), may hold values from -6 to 6
- teacher_gain: float32 [1664], replicated, may hold values from 0.5 to 1.5
- teacher_up: bfloat16 [1664, 4096], P('dp', 'grp'), may hold values from -0.15625 to 0.15625
- teacher_down: bfloat16 [1664, 4096], P('dp', 'grp'), may hold values from -0.09375 to 0.09375
- student_in: bfloat16 [8192, 768], P('dp'), may hold values from -6 to 6
- student_gain: float32 [768], replicated, may hold values from 0.5 to 1.5
- student_up: bfloat16 [768, 1536], P(None, ('grp', 'dp')), may hold values from -0.21875 to 0.21875
- student_down: bfloat16 [1536, 768], P(('grp', 'dp')), may hold values from -0.15625 to 0.15625
- student_head: bfloat16 [768, 1664], P(None, ('grp', 'dp')), may hold values from -0.21875 to 0.21875
- student_proj: bfloat16 [768, 512], P(None, ('grp', 'dp')), may hold values from -1 to 1
- word_table: bfloat16 [49408, 512], P(('grp', 'dp')), may hold values from -6 to 6
- caption_ids: int32 [32, 77], replicated, may hold values from 0 to 49407
- positive: int32 [32], replicated, may hold values from 0 to 31, each once
Outputs:
- loss: float32 [], replicated
- grad_up: float32 [768, 1536], P(None, ('grp', 'dp'))
- grad_down: float32 [1536, 768], P(('grp', 'dp'))
- grad_head: float32 [768, 1664], P(None, ('grp', 'dp'))
- grad_proj: float32 [768, 512], P(None, ('grp', 'dp'))
Inputs may be any that keep to these rules, and one draw needn't show every extreme that they name: Each caption is the positive of exactly one image.
All inputs are finite; a program needn't handle non-finite values.
Results may differ from a plain program's by a relative error of at most 0.0065.
Values may be sent and summed in bfloat16 or wider, within the bound.
No kernel may reach another device: no remote copies, remote signals or barrier semaphores. Data moves between devices by JAX's collectives and lax.ppermute only.
A program may use at most 128 MiB of HBM per device.

v0:
```python
import jax
import jax.numpy as jnp
from jax import lax
from jax.sharding import PartitionSpec as P

CAP_LEN = 77
WINDOW = 7
PATCHES = 256
BOTH = ("grp", "dp")
BF16 = jnp.bfloat16
F32 = jnp.float32


def normalize_rows(values, gain):
    center = values - jnp.mean(values, -1, keepdims=True)
    spread = jnp.mean(center * center, -1, keepdims=True)
    return center * lax.rsqrt(spread + 1e-05) * gain


def gelu_tanh(values):
    return jax.nn.gelu(values, approximate=True)


def unit_rows(values):
    return values / jnp.sqrt(jnp.sum(values * values, -1, keepdims=True) + 1e-06)


def dot(a, b, ca, cb, out=F32):
    return lax.dot_general(a, b, (((ca,), (cb,)), ((), ())), preferred_element_type=F32).astype(out)


def exact(a, b, ca, cb):
    return lax.dot_general(
        a, b, (((ca,), (cb,)), ((), ())), precision=lax.Precision.HIGHEST, preferred_element_type=F32
    )


def pick(values, index, size, axis=0):
    return lax.dynamic_slice_in_dim(values, index * size, size, axis)


def after(values, *first):
    return lax.optimization_barrier((values,) + first)[0]


def local(
    teacher_in,
    teacher_gain,
    teacher_up,
    teacher_down,
    student_in,
    student_gain,
    student_up,
    student_down,
    student_head,
    student_proj,
    word_table,
    caption_ids,
    positive,
):
    grp = lax.axis_index("grp")
    dp = lax.axis_index("dp")
    n_grp = lax.axis_size("grp")
    n_dp = lax.axis_size("dp")
    devices = n_grp * n_dp
    n_z = n_dp // 4
    n_chips = n_dp // 2
    core = dp & 1
    chip = dp >> 1
    y = chip & 1
    z = chip >> 1
    me = grp * n_dp + dp
    MASK_C, MASK_Y, MASK_X = 1, 2, n_dp
    top = chip // n_z
    low = chip & (n_z - 1)

    def swap(values, mask):
        return lax.ppermute(values, BOTH, [(i, i ^ mask) for i in range(devices)])

    line = []

    def queued(values, mask, *first):
        first = first + tuple(line[: len(line) - WINDOW + 1][-6:] if len(line) >= WINDOW else ())
        if first:
            values = after(values, *first)
        line.append(swap(values, mask))
        return line[-1]

    def put(buffer, values, index):
        return lax.dynamic_update_slice(
            buffer, values[None], (index,) + (0,) * (buffer.ndim - 1)
        )

    width = student_in.shape[1]
    n_head = student_head.shape[1]
    tile = n_head + 8 - n_head % 8
    rows_w, hidden_w = teacher_up.shape
    half_w = hidden_w // 2
    at = jnp.arange(2 * tile, dtype=jnp.int32)
    at = jnp.where(at % tile < n_head, (at // tile) * n_head + at % tile, -1)
    widen = (at[:, None] == jnp.arange(rows_w, dtype=jnp.int32)[None, :]).astype(BF16)
    send_up = pick(teacher_up, 1 - core, half_w, 1)
    down_rows = lax.optimization_barrier(dot(widen, teacher_down, 1, 0, BF16))
    send_down = pick(down_rows, 1 - core, half_w, 1)
    far_up, far_down, far_in = swap(send_up, MASK_C), swap(send_down, MASK_C), swap(teacher_in, MASK_C)
    own_up = pick(teacher_up, core, half_w, 1)
    own_down = pick(down_rows, core, half_w, 1)

    def in_order(mine, other):
        return jnp.stack([jnp.where(core == 0, mine, other), jnp.where(core == 0, other, mine)])

    up_pair = in_order(own_up, far_up).reshape(2 * rows_w, half_w)
    down_pair = in_order(own_down, far_down).reshape(4 * tile, half_w)

    n_up = student_up.shape[1]
    n_down = student_down.shape[0]
    n_proj = student_proj.shape[1]
    head_rows = dot(widen[:tile, :n_head], student_head, 1, 1, BF16)
    block = jnp.concatenate(
        [
            after(student_up, send_up, send_down).T,
            student_down,
            student_proj.T,
            head_rows,
        ],
        0,
    )

    half = devices // 2
    place_own = (me ^ (4 * chip)) >> 2
    if n_z == 4:
        rounds = [
            [("z", "s", 3), ("z", "s", 1), ("y", "s", 0), ("y", "u", 0)],
            [("z", "u", 3), ("z", "s", 2), ("y", "s", 3), ("y", "s", 1), ("x", "s", (0,))],
            [("z", "u", 1), ("z", "u", 2), ("y", "s", 2), ("y", "u", 3), ("x", "s", (1, 3))],
            [("z", "d", 3), ("z", "d", 1), ("y", "u", 1), ("y", "u", 2), ("x", "s", (2,))],
            [("c", "s", 0), ("z", "d", 2), ("y", "d", 0), ("y", "d", 1), ("y", "d", 3)],
            [("y", "d", 2)],
        ]
    else:
        some = [("z", p, j) for p in "sud" for j in range(1, n_z)]
        some += [("y", p, j) for p in "sud" for j in range(n_z)]
        some += [("x", "s", (j,)) for j in range(n_z)] + [("c", "s", 0)]
        some += [some.pop(some.index(("y", "d", n_z - 1)))]
        rounds = [some[i : i + 1] for i in range(len(some))]
    held = {("z", "s", 0): block, ("z", "u", 0): up_pair, ("z", "d", 0): down_pair}
    stack, placed = [None], []

    def values_of(axis, name, j):
        if axis == "z" and n_z == 4 and j == 2:
            return held["z", name, 3], 4
        if axis == "z":
            return held["z", name, 0], 4 * j
        if axis == "y":
            return held["z", name, j], MASK_Y
        if axis == "x":
            both = []
            for k in j:
                mine, theirs = held["z", name, k], held["y", name, k]
                both += [jnp.where(y == 0, mine, theirs), jnp.where(y == 0, theirs, mine)]
            held["both", name, j] = jnp.stack(both)
            return held["both", name, j], MASK_X
        return stack[0], MASK_C

    def run(batch, *first):
        todo = [values_of(*item) for item in batch]
        values = lax.optimization_barrier(tuple(v for v, _ in todo) + first)
        came = [swap(v, mask) for v, (_, mask) in zip(values, todo)]
        held.update(zip(batch, came))
        for axis, name, j in batch:
            if axis == "x":
                if stack[0] is None:
                    stack[0] = jnp.zeros((half // 2, 2) + block.shape, BF16)
                placed.extend(j)
                for i, k in enumerate(j):
                    pair = slice(2 * i, 2 * i + 2)
                    stack[0] = put(stack[0], held["both", name, j][pair], place_own ^ k)
                    stack[0] = put(stack[0], held["x", name, j][pair], place_own ^ k ^ n_z)
                if len(placed) == n_z:
                    stack[0] = stack[0].reshape((half,) + block.shape)
        return tuple(came), values[len(batch) :]

    came, _ = run(rounds[0])

    ids, word_rows = after((caption_ids, word_table), came[-1])
    caption_count = caption_ids.shape[0]
    vocab_dev = word_table.shape[0]
    codes = me * vocab_dev + jnp.arange(vocab_dev, dtype=jnp.int32)
    counts = jnp.sum(ids[:, :, None] == codes[None, None, :], 1, dtype=F32).astype(BF16)
    words = dot(counts, word_rows, 1, 0)
    embed = words.shape[1]
    came, _ = run(rounds[1], *came)
    words = after(words, came[min(1, len(came) - 1)])
    words = lax.all_to_all(words.reshape(devices, -1, embed), BOTH, 0, 0)
    caption_own = jnp.sum(words, 0) / CAP_LEN

    t_in = after(jnp.concatenate([teacher_in, far_in], 0), came[-1])
    rows_t, t_width = teacher_in.shape
    own_rows = rows_t // n_grp
    t_rows = normalize_rows(t_in.astype(F32), teacher_gain).astype(BF16)
    came, _ = run(rounds[2], *came)

    own_in = after(pick(teacher_in, grp, own_rows), came[0])
    padded = n_chips * 4 * tile
    place = after(jnp.arange(padded, dtype=jnp.int32), came[0])
    canon = (((place // tile) ^ (4 * chip)) * n_head) + place % tile
    canon = jnp.where(place % tile < n_head, canon, -1)
    order = (jnp.arange(t_width, dtype=jnp.int32)[:, None] == canon[None, :]).astype(BF16)
    t_own = dot(own_in, lax.optimization_barrier(order), 1, 0, BF16)
    half_t = padded // 2
    s_rows = pick(after(student_in, came[0]), grp, own_rows).astype(F32)
    s_normed = normalize_rows(s_rows, student_gain).astype(BF16)
    came, (t_rows, caption_own, *_) = run(rounds[3], t_rows, caption_own, *came)

    ups = jnp.zeros((n_chips,) + up_pair.shape, BF16)
    came, (t_own, s_normed, *_) = run(rounds[4], t_own, s_normed, *came)
    for batch in rounds[5:-1]:
        came, _ = run(batch, *came)
    for k in range(n_z):
        ups = put(ups, held["z", "u", k], chip ^ (2 * k))
        ups = put(ups, held["y", "u", k], chip ^ (2 * k + 1))
    up_all = ups.reshape(t_width, half_w)
    t_act = gelu_tanh(dot(t_rows, up_all, 1, 0)).astype(BF16)
    far_stack = held["c", "s", 0]
    stack = stack[0]

    def rows_of(begin, size):
        part = [v[:, begin : begin + size].reshape(half * size, width) for v in (stack, far_stack)]
        return jnp.concatenate(part, 0)

    up_t = rows_of(0, n_up)
    down_w = rows_of(n_up, n_down)
    gate = dot(s_normed, up_t, 1, 1)
    s_act = gelu_tanh(gate).astype(BF16)
    s_out = s_rows + dot(s_act, down_w, 1, 0)
    s_round = s_out.astype(BF16)
    n_img = own_rows // PATCHES
    pooled = (jnp.sum(s_out.reshape(n_img, PATCHES, width), 1) / PATCHES).astype(BF16)
    sent = jnp.concatenate([pooled.astype(F32).reshape(-1), caption_own.reshape(-1)])

    def second(g):
        span = range(g * n_z // 2, (g + 1) * n_z // 2)
        return jnp.concatenate([w for k in span for w in (held["z", "d", k], held["y", "d", k])], 0)

    kept_rows = []

    def to_owner(g, down_g, far):
        part = (dot(t_act[:rows_t], down_g, 1, 1) + far.astype(F32)).astype(BF16)
        kept_rows.append(pick(part, grp, own_rows))
        return swap(pick(part, 1 - grp, own_rows), MASK_X)

    if n_z == 4:
        down_g = second(0)
        far = swap(dot(t_act[rows_t:], down_g, 1, 1, BF16), MASK_C)
        _, (far, sent, *_) = run(rounds[-1], far, sent, *came)
    else:
        _, (sent, *_) = run(rounds[-1], sent, *came)
        down_g = second(0)
        far = swap(dot(t_act[rows_t:], down_g, 1, 1, BF16), MASK_C)
    others = [to_owner(0, down_g, far)]
    got = lax.all_to_all(jnp.broadcast_to(sent[None], (devices,) + sent.shape), BOTH, 0, 0)

    begin = n_up + n_down + n_proj
    near_h, far_h = stack[:, begin:], after(far_stack, others[0])[:, begin:]
    heads = jnp.stack(
        [jnp.where(core == 0, near_h, far_h), jnp.where(core == 0, far_h, near_h)], 1
    )
    head_g = [heads[g * half // 2 : (g + 1) * half // 2].reshape(half_t, width) for g in range(2)]
    proj_rel = rows_of(n_up + n_down, n_proj)
    place_e = jnp.arange(devices * n_proj, dtype=jnp.int32)
    block_e = place_e // n_proj
    block_e = ((block_e % half) * 2 + ((block_e // half) ^ core)) ^ (4 * chip)
    from_e = block_e * n_proj + place_e % n_proj
    order_e = (place_e[:, None] == from_e[None, :]).astype(BF16)
    proj_t = dot(order_e, proj_rel, 1, 0, BF16)
    preds_s = [dot(s_round, head_g[g], 1, 1) for g in range(2)]

    pooled_all = got[:, : n_img * width].reshape(-1, width).astype(BF16)
    caption = unit_rows(got[:, n_img * width :].reshape(caption_count, embed))
    projected = dot(pooled_all, proj_t, 1, 1)
    proj_norm = jnp.sqrt(jnp.sum(projected * projected, -1, keepdims=True) + 1e-06)
    image = projected / proj_norm
    wanted = jnp.transpose(positive.reshape(n_dp, n_grp, n_img), (1, 0, 2)).reshape(-1)
    match = (wanted[:, None] == jnp.arange(caption_count, dtype=jnp.int32)[None, :]).astype(F32)
    scores = 100.0 * exact(image, caption, 1, 1)
    contrast = (
        jnp.sum(jax.nn.logsumexp(scores, 1))
        + jnp.sum(jax.nn.logsumexp(scores, 0))
        - 2.0 * jnp.sum(match * scores)
    )
    grad_scores = jax.nn.softmax(scores, 1) + jax.nn.softmax(scores, 0) - 2.0 * match
    grad_image = 100.0 * exact(grad_scores, caption, 1, 0)
    grad_projected = (
        (grad_image - image * jnp.sum(image * grad_image, -1, keepdims=True)) / proj_norm
    ).astype(BF16)
    grad_proj = dot(pick(grad_projected, me, n_proj, 1), pooled_all, 0, 0).T
    grad_pooled = dot(pick(grad_projected, me, n_img), proj_t, 1, 0) / PATCHES

    down_g = second(1)
    far = after(dot(t_act[rows_t:], down_g, 1, 1, BF16), others[0])
    others.append(to_owner(1, down_g, swap(far, MASK_C)))
    diffs = []
    for g in range(2):
        target = t_own[:, g * half_t : (g + 1) * half_t].astype(F32) + (
            kept_rows[g].astype(F32) + others[g].astype(F32)
        )
        diffs.append(preds_s[g] - target)
    feature = (jnp.sum(diffs[0] * diffs[0]) + jnp.sum(diffs[1] * diffs[1])) / t_width

    preds = [(2.0 * d / t_width).astype(BF16) for d in diffs]
    half_s = width // 2
    high = feature.astype(BF16).astype(F32)
    mid = (feature - high).astype(BF16).astype(F32)
    rest = feature - high - mid
    at = jnp.arange(width, dtype=jnp.int32)
    term = jnp.where(at % 3 == 0, high, jnp.where(at % 3 == 1, mid, rest))
    term = jnp.where(at // 3 == me, term, 0.0)
    spare = (jnp.arange(half_t, dtype=jnp.int32) % tile == n_head).astype(F32)[:, None]

    def head_part(pred, side):
        value = dot(pred, pick(s_round, side, half_s, 1), 0, 0)
        return value + spare * pick(term, side, half_s)[None, :]

    head_far = [queued(head_part(p, 1 - core).astype(BF16), MASK_C) for p in preds]
    head_parts = [head_part(p, core) + f.astype(F32) for p, f in zip(preds, head_far)]

    def take(sums, index, dim=0):
        return lax.dynamic_index_in_dim(sums, index, dim, False)

    def wide(values):
        return values.astype(F32)

    def flip_z(values, dim):
        shape = values.shape
        pairs = values.astype(BF16).reshape(shape[:dim] + (n_z // 2, 2) + shape[dim + 1 :])
        return jnp.flip(pairs, dim + 1).reshape(shape)

    def send_z(sums):
        if n_z == 4:
            both = jnp.stack([take(sums, z ^ 1 ^ low), take(sums, z ^ 2 ^ low)])
            return queued(both.astype(BF16), 4)
        return [queued(take(sums, z ^ k ^ low).astype(BF16), 4 * k) for k in range(1, n_z)]

    def add_z(sums, others):
        total = take(sums, z ^ low)
        if n_z == 4:
            far = take(sums, z ^ 3 ^ low) + wide(others[1])
            return total + wide(others[0]) + wide(queued(far.astype(BF16), 12))
        for other in others:
            total = total + wide(other)
        return total

    mine = (grp ^ top) == 0
    head_x = queued(jnp.where(mine, head_parts[1], head_parts[0]).astype(BF16), MASK_X)

    grad_out = dot(preds[0], head_g[0], 1, 0) + dot(preds[1], head_g[1], 1, 0)
    grad_out = (
        (grad_out.reshape(n_img, PATCHES, width) + grad_pooled[:, None, :])
        .reshape(-1, width)
        .astype(BF16)
    )

    part = s_act.shape[1] // 2
    down_far = queued(dot(s_act[:, part:], grad_out, 0, 0, BF16), MASK_C)
    grad_act = dot(grad_out, down_w, 1, 1)
    grad_gate = jax.vjp(gelu_tanh, gate)[1](grad_act)[0].astype(BF16)
    up_far = queued(dot(grad_gate[:, part:], s_normed, 0, 0, BF16), MASK_C)
    down = dot(s_act[:, :part], grad_out, 0, 0) + wide(down_far)
    up = dot(grad_gate[:, :part], s_normed, 0, 0) + wide(up_far)
    sums = [up.reshape(2, n_z, 2, n_up, width), down.reshape(2, n_z, 2, n_down, width)]

    def send(values, mask):
        return queued(jnp.concatenate([v.astype(BF16) for v in values], -2), mask)

    def add(values, came):
        return [values[0] + wide(came[..., :n_up, :]), values[1] + wide(came[..., n_up:, :])]

    hid_y = send([flip_z(take(v, 1 - y, 2), 1) for v in sums], MASK_Y)

    head = jnp.where(mine, head_parts[0], head_parts[1]) + wide(head_x)
    head = head.reshape(n_z, 2, 2, tile, half_s)
    head_z = send_z(head)

    sums = add([take(v, y, 2) for v in sums], hid_y)
    hid_x = send([take(v, (1 - grp) ^ top) for v in sums], MASK_X)

    head = add_z(head, head_z)
    head_y = queued(take(head, 1 - y).astype(BF16), MASK_Y)

    sums = add([take(v, grp ^ top) for v in sums], hid_x)
    if n_z == 4:
        near = [jnp.stack([take(v, z ^ 1 ^ low), take(v, z ^ 2 ^ low)]) for v in sums]
        hid_z = send(near, 4)
        far = add([take(v, z ^ 3 ^ low) for v in sums], hid_z[1])
        out = add([take(v, z ^ low) for v in sums], hid_z[0])
        hid_z = send(far, 12)

    head = take(head, y) + wide(head_y)
    kept = take(head, core)
    came = queued(take(head, 1 - core), MASK_C)
    head = jnp.where(
        core == 0, jnp.concatenate([kept, came], 1), jnp.concatenate([came, kept], 1)
    )
    grad_head = head[:n_head].T
    feature = jnp.sum(head[n_head])

    if n_z == 4:
        out = add(out, hid_z)
    else:
        out = [take(v, z ^ low) for v in sums]
        for k in range(1, n_z):
            out = add(out, send([take(v, z ^ k ^ low) for v in sums], 4 * k))
    grad_up, grad_down = out[0].T, out[1]

    loss = (feature + contrast) / (positive.shape[0] * PATCHES)
    return (loss, grad_up, grad_down, grad_head, grad_proj)


def solution(mesh):
    placed = (
        P("dp", None),
        P(),
        P("dp", "grp"),
        P("dp", "grp"),
        P("dp", None),
        P(),
        P(None, BOTH),
        P(BOTH, None),
        P(None, BOTH),
        P(None, BOTH),
        P(BOTH, None),
        P(),
        P(),
    )
    return jax.shard_map(
        local,
        mesh=mesh,
        in_specs=placed,
        out_specs=(
            P(),
            P(None, BOTH),
            P(BOTH, None),
            P(None, BOTH),
            P(None, BOTH),
        ),
        check_vma=False,
    )
```

profile of v0, /device:TPU:0, one launch (start us, length us, event | category | flops | bytes accessed | tf_op | source)
XLA Modules:
  0.0 296.0 jit_solution(5913655098470605968)
XLA Ops:
  10.7 4.7 %collective-permute-start.1 = (bf16[168,768]{1,0:T(8,128)(2,1)}, bf16[168,768]{1,0:T(8,128)(2,1)}, u32[]{:S(2)}, u32[]{:S(2)}) collective-permute-start(bf16[168,768]{1,0:T(8,128)(2,1)} %pad_maximum_fusion.20), channel_id=1, source_target_pairs={{0,12},{1,13},{2,14},{3,15},{4,8},{5,9},{6,10},{7,11},{8,4},{9,5},... | collective-permute-start | bytes 774152 | tf_op jit(solution)/shard_map/ppermute | solution.py:78
  19.3 5.4 %collective-permute-done.3 = bf16[168,768]{1,0:T(8,128)(2,1)S(1)} collective-permute-done((bf16[168,768]{1,0:T(8,128)(2,1)}, bf16[168,768]{1,0:T(8,128)(2,1)S(1)}, u32[]{:S(2)}, u32[]{:S(2)}) %collective-permute-start.3) | collective-permute-done | bytes 258080 | tf_op jit(solution)/shard_map/ppermute | solution.py:78
  28.7 4.4 %collective-permute-done.4 = bf16[208,1024]{1,0:T(8,128)(2,1)} collective-permute-done((bf16[208,1024]{1,0:T(8,128)(2,1)S(1)}, bf16[208,1024]{1,0:T(8,128)(2,1)}, u32[]{:S(2)}, u32[]{:S(2)}) %collective-permute-start.4) | collective-permute-done | bytes 426016 | tf_op jit(solution)/shard_map/ppermute | solution.py:78
  44.8 4.1 %all-to-all-start = ((f32[32,1,512]{2,1,0:T(1,128)}), f32[32,1,512]{2,1,0:T(1,128)S(1)}, u32[]{:S(2)}, u32[]{:S(2)}) async-start(f32[32,1,512]{2,1,0:T(1,128)} %copy.29), calls=%async_computation | async-start | bytes 131072 | tf_op jit(solution)/shard_map/all_to_all | solution.py:194
  52.3 7.8 %all-to-all-done = f32[32,1,512]{2,1,0:T(1,128)S(1)} async-done(((f32[32,1,512]{2,1,0:T(1,128)}), f32[32,1,512]{2,1,0:T(1,128)S(1)}, u32[]{:S(2)}, u32[]{:S(2)}) %all-to-all-start) | async-done | bytes 65568 | tf_op jit(solution)/shard_map/all_to_all | solution.py:194
  70.0 4.0 %collective-permute-done.10 = bf16[208,1024]{1,0:T(8,128)(2,1)S(1)} collective-permute-done((bf16[208,1024]{1,0:T(8,128)(2,1)}, bf16[208,1024]{1,0:T(8,128)(2,1)S(1)}, u32[]{:S(2)}, u32[]{:S(2)}) %collective-permute-start.10) | collective-permute-done | bytes 426016 | tf_op jit(solution)/shard_map/ppermute | solution.py:78
  86.4 6.1 %collective-permute-done.11 = bf16[4,168,768]{2,1,0:T(8,128)(2,1)S(1)} collective-permute-done((bf16[4,168,768]{2,1,0:T(8,128)(2,1)S(1)}, bf16[4,168,768]{2,1,0:T(8,128)(2,1)S(1)}, u32[]{:S(2)}, u32[]{:S(2)}) %collective-permute-start.11) | collective-permute-done | bytes 1032224 | tf_op jit(solution)/shard_map/ppermute | solution.py:78
  99.7 6.4 %collective-permute-done.17 = bf16[2,168,768]{2,1,0:T(8,128)(2,1)S(1)} collective-permute-done((bf16[2,168,768]{2,1,0:T(8,128)(2,1)S(1)}, bf16[2,168,768]{2,1,0:T(8,128)(2,1)S(1)}, u32[]{:S(2)}, u32[]{:S(2)}) %collective-permute-start.17) | collective-permute-done | bytes 516128 | tf_op jit(solution)/shard_map/ppermute | solution.py:78
  106.9 3.9 %collective-permute-done.21 = bf16[208,1024]{1,0:T(8,128)(2,1)S(1)} collective-permute-done((bf16[208,1024]{1,0:T(8,128)(2,1)S(1)}, bf16[208,1024]{1,0:T(8,128)(2,1)S(1)}, u32[]{:S(2)}, u32[]{:S(2)}) %collective-permute-start.21) | collective-permute-done | bytes 426016 | tf_op jit(solution)/shard_map/ppermute | solution.py:78
  110.8 3.8 %collective-permute-done.19 = bf16[224,1024]{1,0:T(8,128)(2,1)S(1)} collective-permute-done((bf16[224,1024]{1,0:T(8,128)(2,1)S(1)}, bf16[224,1024]{1,0:T(8,128)(2,1)S(1)}, u32[]{:S(2)}, u32[]{:S(2)}) %collective-permute-start.19) | collective-permute-done | bytes 458784 | tf_op jit(solution)/shard_map/ppermute | solution.py:78
  121.4 15.8 %fusion.13 = bf16[1024,1024]{1,0:T(8,128)(2,1)S(1)} fusion(bf16[1024,1664]{1,0:T(8,128)(2,1)S(1)} %copy-done.17, bf16[1664,1024]{1,0:T(8,128)(2,1)S(1)} %bitcast.179), kind=kOutput, calls=%fused_computation.18 | convolution fusion | flops 3499098112 | bytes 8912896 | tf_op jit(solution)/shard_map/dot_general | solution.py:29
  143.5 6.4 %collective-permute-done.25 = bf16[224,1024]{1,0:T(8,128)(2,1)S(1)} collective-permute-done((bf16[224,1024]{1,0:T(8,128)(2,1)}, bf16[224,1024]{1,0:T(8,128)(2,1)S(1)}, u32[]{:S(2)}, u32[]{:S(2)}) %collective-permute-start.25) | collective-permute-done | bytes 458784 | tf_op jit(solution)/shard_map/ppermute | solution.py:78
  158.9 3.4 %add_convert_fusion.1 = bf16[512,896]{1,0:T(8,128)(2,1)S(1)} fusion(bf16[512,896]{1,0:T(8,128)(2,1)} %collective-permute-done.26, bf16[1024,1024]{1,0:T(8,128)(2,1)} %copy-done.70, bf16[224,1024]{1,0:T(8,128)(2,1)} %copy-done.69, bf16[224,1024]{1,0:T(8,128)(2,1)} %copy-done.66, bf16[224,1024]{1,0:T(8,128)(2,1)} %copy-done.68, bf16[224,1024]{1,0:T(8,128)(2,1)} %bitcast.199), kind=kOutput, calls=%fused_computation.39 | convolution fusion | flops 948240384 | bytes 4718592 | tf_op jit(solution)/shard_map/dot_general | solution.py:29
  169.9 7.0 %collective-permute-done.29 = bf16[224,1024]{1,0:T(8,128)(2,1)} collective-permute-done((bf16[224,1024]{1,0:T(8,128)(2,1)S(1)}, bf16[224,1024]{1,0:T(8,128)(2,1)}, u32[]{:S(2)}, u32[]{:S(2)}) %collective-permute-start.29) | collective-permute-done | bytes 458784 | tf_op jit(solution)/shard_map/ppermute | solution.py:78
  187.1 11.1 %collective-permute-done.31 = bf16[256,896]{1,0:T(8,128)(2,1)S(1)} collective-permute-done((bf16[256,896]{1,0:T(8,128)(2,1)S(1)}, bf16[256,896]{1,0:T(8,128)(2,1)S(1)}, u32[]{:S(2)}, u32[]{:S(2)}) %collective-permute-start.31) | collective-permute-done | bytes 458784 | tf_op jit(solution)/shard_map/ppermute | solution.py:78
  212.1 2.9 select_convert_fusion
  221.6 3.3 %convert_add_fusion.1 = f32[768,768]{1,0:T(8,128)} fusion(bf16[768,768]{1,0:T(8,128)(2,1)} %collective-permute-done.39, bf16[256,768]{1,0:T(8,128)(2,1)S(1)} %copy-done.11, bf16[256,1536]{1,0:T(8,128)(2,1)} %copy-done.40), kind=kOutput, calls=%fused_computation.30 | convolution fusion | flops 303169536 | bytes 4325376 | tf_op jit(solution)/shard_map/dot_general | solution.py:29
  232.7 3.0 convert_add_fusion.2
  238.3 8.0 %collective-permute-done.35 = bf16[2,2,2,56,384]{4,3,2,1,0:T(8,128)(2,1)S(1)} collective-permute-done((bf16[2,2,2,56,384]{4,3,2,1,0:T(8,128)(2,1)S(1)}, bf16[2,2,2,56,384]{4,3,2,1,0:T(8,128)(2,1)S(1)}, u32[]{:S(2)}, u32[]{:S(2)}) %collective-permute-start.35) | collective-permute-done | bytes 344096 | tf_op jit(solution)/shard_map/ppermute | solution.py:78
  247.3 3.2 %collective-permute-start.36 = (bf16[2,2,56,384]{3,2,1,0:T(8,128)(2,1)S(1)}, bf16[2,2,56,384]{3,2,1,0:T(8,128)(2,1)S(1)}, u32[]{:S(2)}, u32[]{:S(2)}) collective-permute-start(bf16[2,2,56,384]{3,2,1,0:T(8,128)(2,1)S(1)} %fusion.63), channel_id=1, source_target_pairs={{0,12},{1,13},{2,14},{3,15},{4,8},{5,9},{6,10},{7,11},{8,4},{9,5},... | collective-permute-start | bytes 516104 | tf_op jit(solution)/shard_map/ppermute | solution.py:78
  250.5 4.2 %collective-permute-done.36 = bf16[2,2,56,384]{3,2,1,0:T(8,128)(2,1)S(1)} collective-permute-done((bf16[2,2,56,384]{3,2,1,0:T(8,128)(2,1)S(1)}, bf16[2,2,56,384]{3,2,1,0:T(8,128)(2,1)S(1)}, u32[]{:S(2)}, u32[]{:S(2)}) %collective-permute-start.36) | collective-permute-done | bytes 172064 | tf_op jit(solution)/shard_map/ppermute | solution.py:78
  269.0 6.8 %collective-permute-done.42 = bf16[4,96,768]{2,1,0:T(8,128)(2,1)} collective-permute-done((bf16[4,96,768]{2,1,0:T(8,128)(2,1)}, bf16[4,96,768]{2,1,0:T(8,128)(2,1)}, u32[]{:S(2)}, u32[]{:S(2)}) %collective-permute-start.42) | collective-permute-done | bytes 589856 | tf_op jit(solution)/shard_map/ppermute | solution.py:78
  285.8 3.2 %collective-permute-start.44 = (bf16[96,768]{1,0:T(8,128)(2,1)S(1)}, bf16[96,768]{1,0:T(8,128)(2,1)S(1)}, u32[]{:S(2)}, u32[]{:S(2)}) collective-permute-start(bf16[96,768]{1,0:T(8,128)(2,1)S(1)} %pad_maximum_fusion.21), channel_id=1, source_target_pairs={{0,12},{1,13},{2,14},{3,15},{4,8},{5,9},{6,10},{7,11},{8,4},{9,5},... | collective-permute-start | bytes 442376 | tf_op jit(solution)/shard_map/ppermute | solution.py:78
  289.7 3.2 %collective-permute-done.44 = bf16[96,768]{1,0:T(8,128)(2,1)S(1)} collective-permute-done((bf16[96,768]{1,0:T(8,128)(2,1)S(1)}, bf16[96,768]{1,0:T(8,128)(2,1)S(1)}, u32[]{:S(2)}, u32[]{:S(2)}) %collective-permute-start.44) | collective-permute-done | bytes 147488 | tf_op jit(solution)/shard_map/ppermute | solution.py:78
  (360 shorter events, 156.7 us)
Async XLA Ops:
  5.8 74.4 %collective-permute-start.15 = (bf16[512,1664]{1,0:T(8,128)(2,1)}, bf16[512,1664]{1,0:T(8,128)(2,1)}, u32[]{:S(2)}, u32[]{:S(2)}) collective-permute-start(bf16[512,1664]{1,0:T(8,128)(2,1)} %param.13), channel_id=1, source_target_pairs={{0,1},{1,0},{2,3},{3,2},{4,5},{5,4},{6,7},{7,6},{8,9},{9,8},{10,11... | collective-permute-start | bytes 5111816 | tf_op jit(solution)/shard_map/ppermute | solution.py:78
  10.7 23.2 %collective-permute-start.1 = (bf16[168,768]{1,0:T(8,128)(2,1)}, bf16[168,768]{1,0:T(8,128)(2,1)}, u32[]{:S(2)}, u32[]{:S(2)}) collective-permute-start(bf16[168,768]{1,0:T(8,128)(2,1)} %pad_maximum_fusion.20), channel_id=1, source_target_pairs={{0,12},{1,13},{2,14},{3,15},{4,8},{5,9},{6,10},{7,11},{8,4},{9,5},... | collective-permute-start | bytes 774152 | tf_op jit(solution)/shard_map/ppermute | solution.py:78
  15.4 18.5 %collective-permute-start.2 = (bf16[168,768]{1,0:T(8,128)(2,1)}, bf16[168,768]{1,0:T(8,128)(2,1)}, u32[]{:S(2)}, u32[]{:S(2)}) collective-permute-start(bf16[168,768]{1,0:T(8,128)(2,1)} %pad_maximum_fusion.20), channel_id=1, source_target_pairs={{0,4},{1,5},{2,6},{3,7},{4,0},{5,1},{6,2},{7,3},{8,12},{9,13},{10,... | collective-permute-start | bytes 774152 | tf_op jit(solution)/shard_map/ppermute | solution.py:78
  16.9 16.3 %collective-permute-start.4 = (bf16[208,1024]{1,0:T(8,128)(2,1)S(1)}, bf16[208,1024]{1,0:T(8,128)(2,1)}, u32[]{:S(2)}, u32[]{:S(2)}) collective-permute-start(bf16[208,1024]{1,0:T(8,128)(2,1)S(1)} %bitcast.184), channel_id=1, source_target_pairs={{0,2},{1,3},{2,0},{3,1},{4,6},{5,7},{6,4},{7,5},{8,10},{9,11},{10,... | collective-permute-start | bytes 1277960 | tf_op jit(solution)/shard_map/ppermute | solution.py:78
  35.6 13.3 %collective-permute-start.7 = (bf16[168,768]{1,0:T(8,128)(2,1)}, bf16[168,768]{1,0:T(8,128)(2,1)}, u32[]{:S(2)}, u32[]{:S(2)}) collective-permute-start(bf16[168,768]{1,0:T(8,128)(2,1)} %collective-permute-done.2), channel_id=1, source_target_pairs={{0,2},{1,3},{2,0},{3,1},{4,6},{5,7},{6,4},{7,5},{8,10},{9,11},{10,... | collective-permute-start | bytes 774152 | tf_op jit(solution)/shard_map/ppermute | solution.py:78
  37.7 22.5 %collective-permute-start.5 = (bf16[208,1024]{1,0:T(8,128)(2,1)}, bf16[208,1024]{1,0:T(8,128)(2,1)}, u32[]{:S(2)}, u32[]{:S(2)}) collective-permute-start(bf16[208,1024]{1,0:T(8,128)(2,1)} %bitcast.185), channel_id=1, source_target_pairs={{0,12},{1,13},{2,14},{3,15},{4,8},{5,9},{6,10},{7,11},{8,4},{9,5},... | collective-permute-start | bytes 1277960 | tf_op jit(solution)/shard_map/ppermute | solution.py:78
  42.7 17.5 %collective-permute-start.9 = (bf16[2,168,768]{2,1,0:T(8,128)(2,1)}, bf16[2,168,768]{2,1,0:T(8,128)(2,1)}, u32[]{:S(2)}, u32[]{:S(2)}) collective-permute-start(bf16[2,168,768]{2,1,0:T(8,128)(2,1)} %pad_maximum_fusion.13), channel_id=1, source_target_pairs={{0,16},{1,17},{2,18},{3,19},{4,20},{5,21},{6,22},{7,23},{8,24},{9,... | collective-permute-start | bytes 1548296 | tf_op jit(solution)/shard_map/ppermute | solution.py:78
  44.8 15.2 %all-to-all-start = ((f32[32,1,512]{2,1,0:T(1,128)}), f32[32,1,512]{2,1,0:T(1,128)S(1)}, u32[]{:S(2)}, u32[]{:S(2)}) async-start(f32[32,1,512]{2,1,0:T(1,128)} %copy.29), calls=%async_computation | async-start | bytes 131072 | tf_op jit(solution)/shard_map/all_to_all | solution.py:194
  61.4 24.9 %collective-permute-start.14 = (bf16[208,1024]{1,0:T(8,128)(2,1)}, bf16[208,1024]{1,0:T(8,128)(2,1)S(1)}, u32[]{:S(2)}, u32[]{:S(2)}) collective-permute-start(bf16[208,1024]{1,0:T(8,128)(2,1)} %collective-permute-done.5), channel_id=1, source_target_pairs={{0,4},{1,5},{2,6},{3,7},{4,0},{5,1},{6,2},{7,3},{8,12},{9,13},{10,... | collective-permute-start | bytes 1277960 | tf_op jit(solution)/shard_map/ppermute | solution.py:78
  63.1 23.3 %collective-permute-start.16 = (bf16[208,1024]{1,0:T(8,128)(2,1)}, bf16[208,1024]{1,0:T(8,128)(2,1)S(1)}, u32[]{:S(2)}, u32[]{:S(2)}) collective-permute-start(bf16[208,1024]{1,0:T(8,128)(2,1)} %collective-permute-done.5), channel_id=1, source_target_pairs={{0,2},{1,3},{2,0},{3,1},{4,6},{5,7},{6,4},{7,5},{8,10},{9,11},{10,... | collective-permute-start | bytes 1277960 | tf_op jit(solution)/shard_map/ppermute | solution.py:78
  69.3 23.2 %collective-permute-start.11 = (bf16[4,168,768]{2,1,0:T(8,128)(2,1)S(1)}, bf16[4,168,768]{2,1,0:T(8,128)(2,1)S(1)}, u32[]{:S(2)}, u32[]{:S(2)}) collective-permute-start(bf16[4,168,768]{2,1,0:T(8,128)(2,1)S(1)} %copy-done.32), channel_id=1, source_target_pairs={{0,16},{1,17},{2,18},{3,19},{4,20},{5,21},{6,22},{7,23},{8,24},{9,... | collective-permute-start | bytes 3096584 | tf_op jit(solution)/shard_map/ppermute | solution.py:78
  92.4 14.4 %collective-permute-start.20 = (bf16[208,1024]{1,0:T(8,128)(2,1)S(1)}, bf16[208,1024]{1,0:T(8,128)(2,1)S(1)}, u32[]{:S(2)}, u32[]{:S(2)}) collective-permute-start(bf16[208,1024]{1,0:T(8,128)(2,1)S(1)} %collective-permute-done.10), channel_id=1, source_target_pairs={{0,2},{1,3},{2,0},{3,1},{4,6},{5,7},{6,4},{7,5},{8,10},{9,11},{10,... | collective-permute-start | bytes 1277960 | tf_op jit(solution)/shard_map/ppermute | solution.py:78
  92.8 18.0 %collective-permute-start.21 = (bf16[208,1024]{1,0:T(8,128)(2,1)S(1)}, bf16[208,1024]{1,0:T(8,128)(2,1)S(1)}, u32[]{:S(2)}, u32[]{:S(2)}) collective-permute-start(bf16[208,1024]{1,0:T(8,128)(2,1)S(1)} %collective-permute-done.14), channel_id=1, source_target_pairs={{0,2},{1,3},{2,0},{3,1},{4,6},{5,7},{6,4},{7,5},{8,10},{9,11},{10,... | collective-permute-start | bytes 1277960 | tf_op jit(solution)/shard_map/ppermute | solution.py:78
  94.5 16.4 %collective-permute-start.18 = (bf16[224,1024]{1,0:T(8,128)(2,1)S(1)}, bf16[224,1024]{1,0:T(8,128)(2,1)}, u32[]{:S(2)}, u32[]{:S(2)}) collective-permute-start(bf16[224,1024]{1,0:T(8,128)(2,1)S(1)} %bitcast.200), channel_id=1, source_target_pairs={{0,12},{1,13},{2,14},{3,15},{4,8},{5,9},{6,10},{7,11},{8,4},{9,5},... | collective-permute-start | bytes 1376264 | tf_op jit(solution)/shard_map/ppermute | solution.py:78
  95.7 18.9 %collective-permute-start.19 = (bf16[224,1024]{1,0:T(8,128)(2,1)S(1)}, bf16[224,1024]{1,0:T(8,128)(2,1)S(1)}, u32[]{:S(2)}, u32[]{:S(2)}) collective-permute-start(bf16[224,1024]{1,0:T(8,128)(2,1)S(1)} %bitcast.201), channel_id=1, source_target_pairs={{0,4},{1,5},{2,6},{3,7},{4,0},{5,1},{6,2},{7,3},{8,12},{9,13},{10,... | collective-permute-start | bytes 1376264 | tf_op jit(solution)/shard_map/ppermute | solution.py:78
  115.4 35.3 %collective-permute-start.22 = (bf16[16,168,768]{2,1,0:T(8,128)(2,1)}, bf16[16,168,768]{2,1,0:T(8,128)(2,1)}, u32[]{:S(2)}, u32[]{:S(2)}) collective-permute-start(bf16[16,168,768]{2,1,0:T(8,128)(2,1)} %bitcast.26), channel_id=1, source_target_pairs={{0,1},{1,0},{2,3},{3,2},{4,5},{5,4},{6,7},{7,6},{8,9},{9,8},{10,11... | collective-permute-start | bytes 12386312 | tf_op jit(solution)/shard_map/ppermute | solution.py:78
  119.3 22.2 %collective-permute-start.23 = (bf16[224,1024]{1,0:T(8,128)(2,1)S(1)}, bf16[224,1024]{1,0:T(8,128)(2,1)S(1)}, u32[]{:S(2)}, u32[]{:S(2)}) collective-permute-start(bf16[224,1024]{1,0:T(8,128)(2,1)S(1)} %bitcast.202), channel_id=1, source_target_pairs={{0,2},{1,3},{2,0},{3,1},{4,6},{5,7},{6,4},{7,5},{8,10},{9,11},{10,... | collective-permute-start | bytes 1376264 | tf_op jit(solution)/shard_map/ppermute | solution.py:78
  119.7 22.4 %collective-permute-start.24 = (bf16[224,1024]{1,0:T(8,128)(2,1)S(1)}, bf16[224,1024]{1,0:T(8,128)(2,1)S(1)}, u32[]{:S(2)}, u32[]{:S(2)}) collective-permute-start(bf16[224,1024]{1,0:T(8,128)(2,1)S(1)} %copy-done.67), channel_id=1, source_target_pairs={{0,2},{1,3},{2,0},{3,1},{4,6},{5,7},{6,4},{7,5},{8,10},{9,11},{10,... | collective-permute-start | bytes 1376264 | tf_op jit(solution)/shard_map/ppermute | solution.py:78
  141.1 14.5 %collective-permute-start.27 = (bf16[224,1024]{1,0:T(8,128)(2,1)}, bf16[224,1024]{1,0:T(8,128)(2,1)}, u32[]{:S(2)}, u32[]{:S(2)}) collective-permute-start(bf16[224,1024]{1,0:T(8,128)(2,1)} %collective-permute-done.18), channel_id=1, source_target_pairs={{0,2},{1,3},{2,0},{3,1},{4,6},{5,7},{6,4},{7,5},{8,10},{9,11},{10,... | collective-permute-start | bytes 1376264 | tf_op jit(solution)/shard_map/ppermute | solution.py:78
  162.4 18.9 %collective-permute-start.28 = (bf16[256,896]{1,0:T(8,128)(2,1)S(1)}, bf16[256,896]{1,0:T(8,128)(2,1)S(1)}, u32[]{:S(2)}, u32[]{:S(2)}) collective-permute-start(bf16[256,896]{1,0:T(8,128)(2,1)S(1)} %constant_dynamic-slice_fusion.3), channel_id=1, source_target_pairs={{0,16},{1,17},{2,18},{3,19},{4,20},{5,21},{6,22},{7,23},{8,24},{9,... | collective-permute-start | bytes 1376264 | tf_op jit(solution)/shard_map/ppermute | solution.py:78
  185.3 13.0 %collective-permute-start.31 = (bf16[256,896]{1,0:T(8,128)(2,1)S(1)}, bf16[256,896]{1,0:T(8,128)(2,1)S(1)}, u32[]{:S(2)}, u32[]{:S(2)}) collective-permute-start(bf16[256,896]{1,0:T(8,128)(2,1)S(1)} %constant_dynamic-slice_fusion.2), channel_id=1, source_target_pairs={{0,16},{1,17},{2,18},{3,19},{4,20},{5,21},{6,22},{7,23},{8,24},{9,... | collective-permute-start | bytes 1376264 | tf_op jit(solution)/shard_map/ppermute | solution.py:78
  215.0 17.7 %collective-permute-start.34 = (bf16[896,384]{1,0:T(8,128)(2,1)}, bf16[896,384]{1,0:T(8,128)(2,1)}, u32[]{:S(2)}, u32[]{:S(2)}) collective-permute-start(bf16[896,384]{1,0:T(8,128)(2,1)} %get-tuple-element.153), channel_id=1, source_target_pairs={{0,16},{1,17},{2,18},{3,19},{4,20},{5,21},{6,22},{7,23},{8,24},{9,... | collective-permute-start | bytes 2064392 | tf_op jit(solution)/shard_map/ppermute | solution.py:78
  229.5 28.0 %collective-permute-start.40 = (bf16[2,4,96,768]{3,2,1,0:T(8,128)(2,1)}, bf16[2,4,96,768]{3,2,1,0:T(8,128)(2,1)}, u32[]{:S(2)}, u32[]{:S(2)}) collective-permute-start(bf16[2,4,96,768]{3,2,1,0:T(8,128)(2,1)} %pad_maximum_fusion.10), channel_id=1, source_target_pairs={{0,2},{1,3},{2,0},{3,1},{4,6},{5,7},{6,4},{7,5},{8,10},{9,11},{10,... | collective-permute-start | bytes 3538952 | tf_op jit(solution)/shard_map/ppermute | solution.py:78
  261.4 14.5 %collective-permute-start.42 = (bf16[4,96,768]{2,1,0:T(8,128)(2,1)}, bf16[4,96,768]{2,1,0:T(8,128)(2,1)}, u32[]{:S(2)}, u32[]{:S(2)}) collective-permute-start(bf16[4,96,768]{2,1,0:T(8,128)(2,1)} %pad_maximum_fusion.12), channel_id=1, source_target_pairs={{0,16},{1,17},{2,18},{3,19},{4,20},{5,21},{6,22},{7,23},{8,24},{9,... | collective-permute-start | bytes 1769480 | tf_op jit(solution)/shard_map/ppermute | solution.py:78
  (96 other events, 780.6 us)
where the time goes:
time: 299 us; the launch traced here: 296 us
  waiting for transfers between devices  99 us (33%)
  matrix products  53.1 us (18%)
  starting transfers between devices  50 us (17%)
  other arithmetic  46.4 us (16%)
  local copies, waits for them, and re-layouts  40.3 us (13%)
  between operations  7.24 us (2%)
    ppermute x45, waiting for transfers between devices, swap(): return lax.ppermute(values, BOTH, [(i, i ^ mask) for i in range(devices)])  91 us
    dot_general x28, matrix products, dot(): lax.dot_general(a, b, (((ca,), (cb,)), ((), ())), preferred_element_type=...  52.3 us
    ppermute x45, starting transfers between devices, swap(): return lax.ppermute(values, BOTH, [(i, i ^ mask) for i in range(devices)])  43.3 us
    unnamed x150, local copies, waits for them, and re-layouts  8.97 us
    all_to_all x1, waiting for transfers between devices, local(): words = lax.all_to_all(words.reshape(devices, -1, embed), BOTH, 0, 0)  7.78 us
    dynamic_update_slice x12, local copies, waits for them, and re-layouts, put(): lax.dynamic_update_slice(buffer, values[None], (index,) + (0,) * (buffer....  6.98 us
    slice x4, local copies, waits for them, and re-layouts, rows_of(): v[:, begin:begin + size].reshape(half * size, width)  6.19 us
  transfers between devices with their start and end apart: 47, of which 23 were waited for; matrix products, arithmetic and copies ran while one was open for 40% of the time, Pallas kernels for 0%

commit v1 on v0

--- a/solution.py
+++ b/solution.py
@@ -73,6 +73,8 @@
     MASK_C, MASK_Y, MASK_X = 1, 2, n_dp
     top = chip // n_z
     low = chip & (n_z - 1)
+    even = chip - y
+    low_even = even & (n_z - 1)
 
     def swap(values, mask):
         return lax.ppermute(values, BOTH, [(i, i ^ mask) for i in range(devices)])
@@ -127,14 +129,14 @@
     )
 
     half = devices // 2
-    place_own = (me ^ (4 * chip)) >> 2
+    place_own = (me ^ (4 * even)) >> 2
     if n_z == 4:
         rounds = [
             [("z", "s", 3), ("z", "s", 1), ("y", "s", 0), ("y", "u", 0)],
             [("z", "u", 3), ("z", "s", 2), ("y", "s", 3), ("y", "s", 1), ("x", "s", (0,))],
-            [("z", "u", 1), ("z", "u", 2), ("y", "s", 2), ("y", "u", 3), ("x", "s", (1, 3))],
+            [("zz", "u", 1), ("y", "s", 2), ("y", "u", 3), ("x", "s", (1, 3)), ("y", "d", 0)],
             [("z", "d", 3), ("z", "d", 1), ("y", "u", 1), ("y", "u", 2), ("x", "s", (2,))],
-            [("c", "s", 0), ("z", "d", 2), ("y", "d", 0), ("y", "d", 1), ("y", "d", 3)],
+            [("c", "s", 0), ("z", "d", 2), ("y", "d", 1), ("y", "d", 3)],
             [("y", "d", 2)],
         ]
     else:
@@ -147,6 +149,8 @@
     stack, placed = [None], []
 
     def values_of(axis, name, j):
+        if axis == "zz":
+            return jnp.stack([held["z", name, 0], held["z", name, 3]]), 4
         if axis == "z" and n_z == 4 and j == 2:
             return held["z", name, 3], 4
         if axis == "z":
@@ -168,6 +172,8 @@
         came = [swap(v, mask) for v, (_, mask) in zip(values, todo)]
         held.update(zip(batch, came))
         for axis, name, j in batch:
+            if axis == "zz":
+                held["z", name, 1], held["z", name, 2] = held[axis, name, j]
             if axis == "x":
                 if stack[0] is None:
                     stack[0] = jnp.zeros((half // 2, 2) + block.shape, BF16)
@@ -265,11 +271,15 @@
     heads = jnp.stack(
         [jnp.where(core == 0, near_h, far_h), jnp.where(core == 0, far_h, near_h)], 1
     )
+    heads = heads.reshape((n_chips // 2, 2, 2) + heads.shape[1:])
+    heads = jnp.stack(
+        [jnp.where(y == 0, heads[:, i], heads[:, 1 - i]) for i in range(2)], 1
+    ).reshape((half,) + heads.shape[3:])
     head_g = [heads[g * half // 2 : (g + 1) * half // 2].reshape(half_t, width) for g in range(2)]
     proj_rel = rows_of(n_up + n_down, n_proj)
     place_e = jnp.arange(devices * n_proj, dtype=jnp.int32)
     block_e = place_e // n_proj
-    block_e = ((block_e % half) * 2 + ((block_e // half) ^ core)) ^ (4 * chip)
+    block_e = ((block_e % half) * 2 + ((block_e // half) ^ core)) ^ (4 * even)
     from_e = block_e * n_proj + place_e % n_proj
     order_e = (place_e[:, None] == from_e[None, :]).astype(BF16)
     proj_t = dot(order_e, proj_rel, 1, 0, BF16)
@@ -330,11 +340,6 @@
     def wide(values):
         return values.astype(F32)
 
-    def flip_z(values, dim):
-        shape = values.shape
-        pairs = values.astype(BF16).reshape(shape[:dim] + (n_z // 2, 2) + shape[dim + 1 :])
-        return jnp.flip(pairs, dim + 1).reshape(shape)
-
     def send_z(sums):
         if n_z == 4:
             both = jnp.stack([take(sums, z ^ 1 ^ low), take(sums, z ^ 2 ^ low)])
@@ -375,7 +380,7 @@
     def add(values, came):
         return [values[0] + wide(came[..., :n_up, :]), values[1] + wide(came[..., n_up:, :])]
 
-    hid_y = send([flip_z(take(v, 1 - y, 2), 1) for v in sums], MASK_Y)
+    hid_y = send([take(v, 1 - y, 2) for v in sums], MASK_Y)
 
     head = jnp.where(mine, head_parts[0], head_parts[1]) + wide(head_x)
     head = head.reshape(n_z, 2, 2, tile, half_s)
@@ -389,10 +394,10 @@
 
     sums = add([take(v, grp ^ top) for v in sums], hid_x)
     if n_z == 4:
-        near = [jnp.stack([take(v, z ^ 1 ^ low), take(v, z ^ 2 ^ low)]) for v in sums]
+        near = [jnp.stack([take(v, z ^ 1 ^ low_even), take(v, z ^ 2 ^ low_even)]) for v in sums]
         hid_z = send(near, 4)
-        far = add([take(v, z ^ 3 ^ low) for v in sums], hid_z[1])
-        out = add([take(v, z ^ low) for v in sums], hid_z[0])
+        far = add([take(v, z ^ 3 ^ low_even) for v in sums], hid_z[1])
+        out = add([take(v, z ^ low_even) for v in sums], hid_z[0])
         hid_z = send(far, 12)
 
     head = take(head, y) + wide(head_y)
@@ -407,9 +412,9 @@
     if n_z == 4:
         out = add(out, hid_z)
     else:
-        out = [take(v, z ^ low) for v in sums]
+        out = [take(v, z ^ low_even) for v in sums]
         for k in range(1, n_z):
-            out = add(out, send([take(v, z ^ k ^ low) for v in sums], 4 * k))
+            out = add(out, send([take(v, z ^ k ^ low_even) for v in sums], 4 * k))
     grad_up, grad_down = out[0].T, out[1]
 
     loss = (feature + contrast) / (positive.shape[0] * PATCHES)

time: 299 us -> 293 us (0.980)
  matrix products: 53.1 us -> 40.5 us
  waiting for transfers between devices: 99 us -> 105 us
    dot_general x28, matrix products: 52.3 us -> 39.7 us  [dot(): lax.dot_general(a, b, (((ca,), (cb,)), ((), ())), preferred_element_type=...]
    dynamic_update_slice x12, local copies, waits for them, and re-layouts: 6.98 us -> 11 us  [put(): lax.dynamic_update_slice(buffer, values[None], (index,) + (0,) * (buffer....]
    ppermute x45 -> x44, waiting for transfers between devices: 91 us -> 94.9 us  [swap(): return lax.ppermute(values, BOTH, [(i, i ^ mask) for i in range(devices)])]
    ppermute x45 -> x44, starting transfers between devices: 43.3 us -> 41.7 us  [swap(): return lax.ppermute(values, BOTH, [(i, i ^ mask) for i in range(devices)])]
    unnamed x150 -> x144, local copies, waits for them, and re-layouts: 8.97 us -> 8.87 us
  transfers between devices with their start and end apart: 47 -> 46, of which waited for: 23 -> 22; matrix products, arithmetic and copies ran while one was open for 40% -> 36% of each run, Pallas kernels for 0% -> 0%
where the time goes in v1:
time: 293 us; the launch traced here: 288 us
  waiting for transfers between devices  105 us (36%)
  starting transfers between devices  49.3 us (17%)
  other arithmetic  43.9 us (15%)
  local copies, waits for them, and re-layouts  41.6 us (14%)
  matrix products  40.5 us (14%)
  between operations  7.35 us (3%)
    ppermute x44, waiting for transfers between devices, swap(): return lax.ppermute(values, BOTH, [(i, i ^ mask) for i in range(devices)])  94.9 us
    ppermute x44, starting transfers between devices, swap(): return lax.ppermute(values, BOTH, [(i, i ^ mask) for i in range(devices)])  41.7 us
    dot_general x28, matrix products, dot(): lax.dot_general(a, b, (((ca,), (cb,)), ((), ())), preferred_element_type=...  39.7 us
    dynamic_update_slice x12, local copies, waits for them, and re-layouts, put(): lax.dynamic_update_slice(buffer, values[None], (index,) + (0,) * (buffer....  11 us
    all_to_all x1, waiting for transfers between devices, local(): words = lax.all_to_all(words.reshape(devices, -1, embed), BOTH, 0, 0)  9.91 us
    unnamed x144, local copies, waits for them, and re-layouts  8.87 us
    slice x4, local copies, waits for them, and re-layouts, rows_of(): v[:, begin:begin + size].reshape(half * size, width)  6.43 us
  transfers between devices with their start and end apart: 46, of which 22 were waited for; matrix products, arithmetic and copies ran while one was open for 36% of the time, Pallas kernels for 0%

profile of v1, /device:TPU:0, one launch (start us, length us, event | category | flops | bytes accessed | tf_op | source)
XLA Modules:
  0.0 287.6 jit_solution(12729625251780121623)
XLA Ops:
  10.7 4.7 %collective-permute-start.1 = (bf16[168,768]{1,0:T(8,128)(2,1)}, bf16[168,768]{1,0:T(8,128)(2,1)S(1)}, u32[]{:S(2)}, u32[]{:S(2)}) collective-permute-start(bf16[168,768]{1,0:T(8,128)(2,1)} %pad_maximum_fusion.22), channel_id=1, source_target_pairs={{0,12},{1,13},{2,14},{3,15},{4,8},{5,9},{6,10},{7,11},{8,4},{9,5},... | collective-permute-start | bytes 774152 | tf_op jit(solution)/shard_map/ppermute | solution.py:80
  28.7 4.3 %collective-permute-done.4 = bf16[208,1024]{1,0:T(8,128)(2,1)S(1)} collective-permute-done((bf16[208,1024]{1,0:T(8,128)(2,1)S(1)}, bf16[208,1024]{1,0:T(8,128)(2,1)S(1)}, u32[]{:S(2)}, u32[]{:S(2)}) %collective-permute-start.4) | collective-permute-done | bytes 426016 | tf_op jit(solution)/shard_map/ppermute | solution.py:80
  44.1 3.9 %all-to-all-start = ((f32[32,1,512]{2,1,0:T(1,128)}), f32[32,1,512]{2,1,0:T(1,128)S(1)}, u32[]{:S(2)}, u32[]{:S(2)}) async-start(f32[32,1,512]{2,1,0:T(1,128)} %copy.34), calls=%async_computation | async-start | bytes 131072 | tf_op jit(solution)/shard_map/all_to_all | solution.py:200
  49.3 9.9 %all-to-all-done = f32[32,1,512]{2,1,0:T(1,128)S(1)} async-done(((f32[32,1,512]{2,1,0:T(1,128)}), f32[32,1,512]{2,1,0:T(1,128)S(1)}, u32[]{:S(2)}, u32[]{:S(2)}) %all-to-all-start) | async-done | bytes 65568 | tf_op jit(solution)/shard_map/all_to_all | solution.py:200
  65.4 3.4 %collective-permute-done.13 = bf16[168,768]{1,0:T(8,128)(2,1)S(1)} collective-permute-done((bf16[168,768]{1,0:T(8,128)(2,1)}, bf16[168,768]{1,0:T(8,128)(2,1)S(1)}, u32[]{:S(2)}, u32[]{:S(2)}) %collective-permute-start.13) | collective-permute-done | bytes 258080 | tf_op jit(solution)/shard_map/ppermute | solution.py:80
  73.7 2.8 fusion.5
  76.6 5.6 %collective-permute-done.11 = bf16[2,208,1024]{2,1,0:T(8,128)(2,1)S(1)} collective-permute-done((bf16[2,208,1024]{2,1,0:T(8,128)(2,1)S(1)}, bf16[2,208,1024]{2,1,0:T(8,128)(2,1)S(1)}, u32[]{:S(2)}, u32[]{:S(2)}) %collective-permute-start.11) | collective-permute-done | bytes 852000 | tf_op jit(solution)/shard_map/ppermute | solution.py:80
  86.5 2.8 convolution_convert_fusion
  99.1 6.4 %collective-permute-done.17 = bf16[2,168,768]{2,1,0:T(8,128)(2,1)S(1)} collective-permute-done((bf16[2,168,768]{2,1,0:T(8,128)(2,1)S(1)}, bf16[2,168,768]{2,1,0:T(8,128)(2,1)S(1)}, u32[]{:S(2)}, u32[]{:S(2)}) %collective-permute-start.17) | collective-permute-done | bytes 516128 | tf_op jit(solution)/shard_map/ppermute | solution.py:80
  106.3 3.9 %collective-permute-done.21 = bf16[208,1024]{1,0:T(8,128)(2,1)S(1)} collective-permute-done((bf16[208,1024]{1,0:T(8,128)(2,1)S(1)}, bf16[208,1024]{1,0:T(8,128)(2,1)S(1)}, u32[]{:S(2)}, u32[]{:S(2)}) %collective-permute-start.21) | collective-permute-done | bytes 426016 | tf_op jit(solution)/shard_map/ppermute | solution.py:80
  110.3 3.8 %collective-permute-done.19 = bf16[224,1024]{1,0:T(8,128)(2,1)S(1)} collective-permute-done((bf16[224,1024]{1,0:T(8,128)(2,1)S(1)}, bf16[224,1024]{1,0:T(8,128)(2,1)S(1)}, u32[]{:S(2)}, u32[]{:S(2)}) %collective-permute-start.19) | collective-permute-done | bytes 458784 | tf_op jit(solution)/shard_map/ppermute | solution.py:80
  120.0 7.2 %fusion.13 = bf16[1024,1024]{1,0:T(8,128)(2,1)S(1)} fusion(bf16[1024,1664]{1,0:T(8,128)(2,1)S(1)} %copy-done.15, bf16[1664,1024]{1,0:T(8,128)(2,1)} %bitcast.39), kind=kOutput, calls=%fused_computation.18 | convolution fusion | flops 3499098112 | bytes 8912896 | tf_op jit(solution)/shard_map/dot_general | solution.py:29
  134.6 5.6 %collective-permute-done.24 = bf16[224,1024]{1,0:T(8,128)(2,1)S(1)} collective-permute-done((bf16[224,1024]{1,0:T(8,128)(2,1)}, bf16[224,1024]{1,0:T(8,128)(2,1)S(1)}, u32[]{:S(2)}, u32[]{:S(2)}) %collective-permute-start.24) | collective-permute-done | bytes 458784 | tf_op jit(solution)/shard_map/ppermute | solution.py:80
  146.7 3.7 %all-to-all-start.1 = ((f32[32,1,1280]{2,1,0:T(1,128)}), f32[32,1,1280]{2,1,0:T(1,128)S(1)}, u32[]{:S(2)}, u32[]{:S(2)}) async-start(f32[32,1,1280]{2,1,0:T(1,128)} %broadcast_in_dim.117), calls=%async_computation.1 | async-start | bytes 327680 | tf_op jit(solution)/shard_map/all_to_all | solution.py:267
  150.4 3.4 %add_convert_fusion.1 = bf16[512,896]{1,0:T(8,128)(2,1)S(1)} fusion(bf16[512,896]{1,0:T(8,128)(2,1)} %collective-permute-done.25, bf16[1024,1024]{1,0:T(8,128)(2,1)} %copy-done.67, bf16[224,1024]{1,0:T(8,128)(2,1)} %copy-done.66, bf16[224,1024]{1,0:T(8,128)(2,1)} %copy-done.64, bf16[224,1024]{1,0:T(8,128)(2,1)} %copy-done.62, bf16[224,1024]{1,0:T(8,128)(2,1)} %bitcast.204), kind=kOutput, calls=%fused_computation.41 | convolution fusion | flops 948240384 | bytes 4718592 | tf_op jit(solution)/shard_map/dot_general | solution.py:29
  161.5 6.9 %collective-permute-done.28 = bf16[224,1024]{1,0:T(8,128)(2,1)} collective-permute-done((bf16[224,1024]{1,0:T(8,128)(2,1)S(1)}, bf16[224,1024]{1,0:T(8,128)(2,1)}, u32[]{:S(2)}, u32[]{:S(2)}) %collective-permute-start.28) | collective-permute-done | bytes 458784 | tf_op jit(solution)/shard_map/ppermute | solution.py:80
  179.0 11.1 %collective-permute-done.30 = bf16[256,896]{1,0:T(8,128)(2,1)S(1)} collective-permute-done((bf16[256,896]{1,0:T(8,128)(2,1)S(1)}, bf16[256,896]{1,0:T(8,128)(2,1)S(1)}, u32[]{:S(2)}, u32[]{:S(2)}) %collective-permute-start.30) | collective-permute-done | bytes 458784 | tf_op jit(solution)/shard_map/ppermute | solution.py:80
  212.6 10.5 %collective-permute-done.33 = bf16[896,384]{1,0:T(8,128)(2,1)S(1)} collective-permute-done((bf16[896,384]{1,0:T(8,128)(2,1)S(1)}, bf16[896,384]{1,0:T(8,128)(2,1)S(1)}, u32[]{:S(2)}, u32[]{:S(2)}) %collective-permute-start.33) | collective-permute-done | bytes 688160 | tf_op jit(solution)/shard_map/ppermute | solution.py:80
  227.7 8.7 %collective-permute-done.34 = bf16[2,2,2,56,384]{4,3,2,1,0:T(8,128)(2,1)} collective-permute-done((bf16[2,2,2,56,384]{4,3,2,1,0:T(8,128)(2,1)}, bf16[2,2,2,56,384]{4,3,2,1,0:T(8,128)(2,1)}, u32[]{:S(2)}, u32[]{:S(2)}) %collective-permute-start.34) | collective-permute-done | bytes 344096 | tf_op jit(solution)/shard_map/ppermute | solution.py:80
  238.2 3.1 %collective-permute-start.35 = (bf16[2,2,56,384]{3,2,1,0:T(8,128)(2,1)}, bf16[2,2,56,384]{3,2,1,0:T(8,128)(2,1)}, u32[]{:S(2)}, u32[]{:S(2)}) collective-permute-start(bf16[2,2,56,384]{3,2,1,0:T(8,128)(2,1)} %fusion.66), channel_id=1, source_target_pairs={{0,12},{1,13},{2,14},{3,15},{4,8},{5,9},{6,10},{7,11},{8,4},{9,5},... | collective-permute-start | bytes 516104 | tf_op jit(solution)/shard_map/ppermute | solution.py:80
  241.3 4.5 %collective-permute-done.35 = bf16[2,2,56,384]{3,2,1,0:T(8,128)(2,1)} collective-permute-done((bf16[2,2,56,384]{3,2,1,0:T(8,128)(2,1)}, bf16[2,2,56,384]{3,2,1,0:T(8,128)(2,1)}, u32[]{:S(2)}, u32[]{:S(2)}) %collective-permute-start.35) | collective-permute-done | bytes 172064 | tf_op jit(solution)/shard_map/ppermute | solution.py:80
  257.6 6.5 %collective-permute-done.41 = bf16[4,96,768]{2,1,0:T(8,128)(2,1)} collective-permute-done((bf16[4,96,768]{2,1,0:T(8,128)(2,1)}, bf16[4,96,768]{2,1,0:T(8,128)(2,1)}, u32[]{:S(2)}, u32[]{:S(2)}) %collective-permute-start.41) | collective-permute-done | bytes 589856 | tf_op jit(solution)/shard_map/ppermute | solution.py:80
  267.3 3.9 %collective-permute-start.42 = (bf16[2,96,768]{2,1,0:T(8,128)(2,1)S(1)}, bf16[2,96,768]{2,1,0:T(8,128)(2,1)S(1)}, u32[]{:S(2)}, u32[]{:S(2)}) collective-permute-start(bf16[2,96,768]{2,1,0:T(8,128)(2,1)S(1)} %maximum_maximum_fusion), channel_id=1, source_target_pairs={{0,4},{1,5},{2,6},{3,7},{4,0},{5,1},{6,2},{7,3},{8,12},{9,13},{10,... | collective-permute-start | bytes 884744 | tf_op jit(solution)/shard_map/ppermute | solution.py:80
  278.9 5.5 %collective-permute-done.43 = bf16[96,768]{1,0:T(8,128)(2,1)S(1)} collective-permute-done((bf16[96,768]{1,0:T(8,128)(2,1)S(1)}, bf16[96,768]{1,0:T(8,128)(2,1)S(1)}, u32[]{:S(2)}, u32[]{:S(2)}) %collective-permute-start.43) | collective-permute-done | bytes 147488 | tf_op jit(solution)/shard_map/ppermute | solution.py:80
  (352 shorter events, 148.1 us)
Async XLA Ops:
  5.8 14.1 %collective-permute-start.9 = (bf16[112,1024]{1,0:T(8,128)(2,1)}, bf16[112,1024]{1,0:T(8,128)(2,1)}, u32[]{:S(2)}, u32[]{:S(2)}) collective-permute-start(bf16[112,1024]{1,0:T(8,128)(2,1)} %constant_dynamic-slice_fusion.5), channel_id=1, source_target_pairs={{0,1},{1,0},{2,3},{3,2},{4,5},{5,4},{6,7},{7,6},{8,9},{9,8},{10,11... | collective-permute-start | bytes 688136 | tf_op jit(solution)/shard_map/ppermute | solution.py:80
  5.8 64.6 %collective-permute-start.14 = (bf16[512,1664]{1,0:T(8,128)(2,1)}, bf16[512,1664]{1,0:T(8,128)(2,1)}, u32[]{:S(2)}, u32[]{:S(2)}) collective-permute-start(bf16[512,1664]{1,0:T(8,128)(2,1)} %param.13), channel_id=1, source_target_pairs={{0,1},{1,0},{2,3},{3,2},{4,5},{5,4},{6,7},{7,6},{8,9},{9,8},{10,11... | collective-permute-start | bytes 5111816 | tf_op jit(solution)/shard_map/ppermute | solution.py:80
  10.7 22.5 %collective-permute-start.1 = (bf16[168,768]{1,0:T(8,128)(2,1)}, bf16[168,768]{1,0:T(8,128)(2,1)S(1)}, u32[]{:S(2)}, u32[]{:S(2)}) collective-permute-start(bf16[168,768]{1,0:T(8,128)(2,1)} %pad_maximum_fusion.22), channel_id=1, source_target_pairs={{0,12},{1,13},{2,14},{3,15},{4,8},{5,9},{6,10},{7,11},{8,4},{9,5},... | collective-permute-start | bytes 774152 | tf_op jit(solution)/shard_map/ppermute | solution.py:80
  15.4 17.8 %collective-permute-start.2 = (bf16[168,768]{1,0:T(8,128)(2,1)}, bf16[168,768]{1,0:T(8,128)(2,1)}, u32[]{:S(2)}, u32[]{:S(2)}) collective-permute-start(bf16[168,768]{1,0:T(8,128)(2,1)} %pad_maximum_fusion.22), channel_id=1, source_target_pairs={{0,4},{1,5},{2,6},{3,7},{4,0},{5,1},{6,2},{7,3},{8,12},{9,13},{10,... | collective-permute-start | bytes 774152 | tf_op jit(solution)/shard_map/ppermute | solution.py:80
  19.9 13.2 %collective-permute-start.4 = (bf16[208,1024]{1,0:T(8,128)(2,1)S(1)}, bf16[208,1024]{1,0:T(8,128)(2,1)S(1)}, u32[]{:S(2)}, u32[]{:S(2)}) collective-permute-start(bf16[208,1024]{1,0:T(8,128)(2,1)S(1)} %bitcast.188), channel_id=1, source_target_pairs={{0,2},{1,3},{2,0},{3,1},{4,6},{5,7},{6,4},{7,5},{8,10},{9,11},{10,... | collective-permute-start | bytes 1277960 | tf_op jit(solution)/shard_map/ppermute | solution.py:80
  37.0 22.2 %collective-permute-start.5 = (bf16[208,1024]{1,0:T(8,128)(2,1)S(1)}, bf16[208,1024]{1,0:T(8,128)(2,1)S(1)}, u32[]{:S(2)}, u32[]{:S(2)}) collective-permute-start(bf16[208,1024]{1,0:T(8,128)(2,1)S(1)} %bitcast.189), channel_id=1, source_target_pairs={{0,12},{1,13},{2,14},{3,15},{4,8},{5,9},{6,10},{7,11},{8,4},{9,5},... | collective-permute-start | bytes 1277960 | tf_op jit(solution)/shard_map/ppermute | solution.py:80
  41.9 17.4 %collective-permute-start.10 = (bf16[2,168,768]{2,1,0:T(8,128)(2,1)}, bf16[2,168,768]{2,1,0:T(8,128)(2,1)}, u32[]{:S(2)}, u32[]{:S(2)}) collective-permute-start(bf16[2,168,768]{2,1,0:T(8,128)(2,1)} %pad_maximum_fusion.15), channel_id=1, source_target_pairs={{0,16},{1,17},{2,18},{3,19},{4,20},{5,21},{6,22},{7,23},{8,24},{9,... | collective-permute-start | bytes 1548296 | tf_op jit(solution)/shard_map/ppermute | solution.py:80
  44.1 15.1 %all-to-all-start = ((f32[32,1,512]{2,1,0:T(1,128)}), f32[32,1,512]{2,1,0:T(1,128)S(1)}, u32[]{:S(2)}, u32[]{:S(2)}) async-start(f32[32,1,512]{2,1,0:T(1,128)} %copy.34), calls=%async_computation | async-start | bytes 131072 | tf_op jit(solution)/shard_map/all_to_all | solution.py:200
  60.3 29.0 %collective-permute-start.15 = (bf16[208,1024]{1,0:T(8,128)(2,1)S(1)}, bf16[208,1024]{1,0:T(8,128)(2,1)S(1)}, u32[]{:S(2)}, u32[]{:S(2)}) collective-permute-start(bf16[208,1024]{1,0:T(8,128)(2,1)S(1)} %collective-permute-done.5), channel_id=1, source_target_pairs={{0,2},{1,3},{2,0},{3,1},{4,6},{5,7},{6,4},{7,5},{8,10},{9,11},{10,... | collective-permute-start | bytes 1277960 | tf_op jit(solution)/shard_map/ppermute | solution.py:80
  61.5 27.8 %collective-permute-start.16 = (bf16[224,1024]{1,0:T(8,128)(2,1)}, bf16[224,1024]{1,0:T(8,128)(2,1)S(1)}, u32[]{:S(2)}, u32[]{:S(2)}) collective-permute-start(bf16[224,1024]{1,0:T(8,128)(2,1)} %bitcast.203), channel_id=1, source_target_pairs={{0,2},{1,3},{2,0},{3,1},{4,6},{5,7},{6,4},{7,5},{8,10},{9,11},{10,... | collective-permute-start | bytes 1376264 | tf_op jit(solution)/shard_map/ppermute | solution.py:80
  62.3 19.9 %collective-permute-start.11 = (bf16[2,208,1024]{2,1,0:T(8,128)(2,1)S(1)}, bf16[2,208,1024]{2,1,0:T(8,128)(2,1)S(1)}, u32[]{:S(2)}, u32[]{:S(2)}) collective-permute-start(bf16[2,208,1024]{2,1,0:T(8,128)(2,1)S(1)} %pad_maximum_fusion.13), channel_id=1, source_target_pairs={{0,4},{1,5},{2,6},{3,7},{4,0},{5,1},{6,2},{7,3},{8,12},{9,13},{10,... | collective-permute-start | bytes 2555912 | tf_op jit(solution)/shard_map/ppermute | solution.py:80
  68.7 23.2 %collective-permute-start.12 = (bf16[4,168,768]{2,1,0:T(8,128)(2,1)S(1)}, bf16[4,168,768]{2,1,0:T(8,128)(2,1)S(1)}, u32[]{:S(2)}, u32[]{:S(2)}) collective-permute-start(bf16[4,168,768]{2,1,0:T(8,128)(2,1)S(1)} %pad_maximum_fusion.12), channel_id=1, source_target_pairs={{0,16},{1,17},{2,18},{3,19},{4,20},{5,21},{6,22},{7,23},{8,24},{9,... | collective-permute-start | bytes 3096584 | tf_op jit(solution)/shard_map/ppermute | solution.py:80
  91.9 14.4 %collective-permute-start.20 = (bf16[208,1024]{1,0:T(8,128)(2,1)S(1)}, bf16[208,1024]{1,0:T(8,128)(2,1)S(1)}, u32[]{:S(2)}, u32[]{:S(2)}) collective-permute-start(bf16[208,1024]{1,0:T(8,128)(2,1)S(1)} %get-tuple-element.76), channel_id=1, source_target_pairs={{0,2},{1,3},{2,0},{3,1},{4,6},{5,7},{6,4},{7,5},{8,10},{9,11},{10,... | collective-permute-start | bytes 1277960 | tf_op jit(solution)/shard_map/ppermute | solution.py:80
  92.3 18.0 %collective-permute-start.21 = (bf16[208,1024]{1,0:T(8,128)(2,1)S(1)}, bf16[208,1024]{1,0:T(8,128)(2,1)S(1)}, u32[]{:S(2)}, u32[]{:S(2)}) collective-permute-start(bf16[208,1024]{1,0:T(8,128)(2,1)S(1)} %get-tuple-element.77), channel_id=1, source_target_pairs={{0,2},{1,3},{2,0},{3,1},{4,6},{5,7},{6,4},{7,5},{8,10},{9,11},{10,... | collective-permute-start | bytes 1277960 | tf_op jit(solution)/shard_map/ppermute | solution.py:80
  93.9 16.4 %collective-permute-start.18 = (bf16[224,1024]{1,0:T(8,128)(2,1)S(1)}, bf16[224,1024]{1,0:T(8,128)(2,1)}, u32[]{:S(2)}, u32[]{:S(2)}) collective-permute-start(bf16[224,1024]{1,0:T(8,128)(2,1)S(1)} %bitcast.205), channel_id=1, source_target_pairs={{0,12},{1,13},{2,14},{3,15},{4,8},{5,9},{6,10},{7,11},{8,4},{9,5},... | collective-permute-start | bytes 1376264 | tf_op jit(solution)/shard_map/ppermute | solution.py:80
  95.1 18.9 %collective-permute-start.19 = (bf16[224,1024]{1,0:T(8,128)(2,1)S(1)}, bf16[224,1024]{1,0:T(8,128)(2,1)S(1)}, u32[]{:S(2)}, u32[]{:S(2)}) collective-permute-start(bf16[224,1024]{1,0:T(8,128)(2,1)S(1)} %bitcast.206), channel_id=1, source_target_pairs={{0,4},{1,5},{2,6},{3,7},{4,0},{5,1},{6,2},{7,3},{8,12},{9,13},{10,... | collective-permute-start | bytes 1376264 | tf_op jit(solution)/shard_map/ppermute | solution.py:80
  114.9 26.3 %collective-permute-start.22 = (bf16[16,168,768]{2,1,0:T(8,128)(2,1)}, bf16[16,168,768]{2,1,0:T(8,128)(2,1)}, u32[]{:S(2)}, u32[]{:S(2)}) collective-permute-start(bf16[16,168,768]{2,1,0:T(8,128)(2,1)} %bitcast.30), channel_id=1, source_target_pairs={{0,1},{1,0},{2,3},{3,2},{4,5},{5,4},{6,7},{7,6},{8,9},{9,8},{10,11... | collective-permute-start | bytes 12386312 | tf_op jit(solution)/shard_map/ppermute | solution.py:80
  119.7 13.5 %collective-permute-start.23 = (bf16[224,1024]{1,0:T(8,128)(2,1)S(1)}, bf16[224,1024]{1,0:T(8,128)(2,1)S(1)}, u32[]{:S(2)}, u32[]{:S(2)}) collective-permute-start(bf16[224,1024]{1,0:T(8,128)(2,1)S(1)} %copy-done.65), channel_id=1, source_target_pairs={{0,2},{1,3},{2,0},{3,1},{4,6},{5,7},{6,4},{7,5},{8,10},{9,11},{10,... | collective-permute-start | bytes 1376264 | tf_op jit(solution)/shard_map/ppermute | solution.py:80
  131.4 14.5 %collective-permute-start.26 = (bf16[224,1024]{1,0:T(8,128)(2,1)}, bf16[224,1024]{1,0:T(8,128)(2,1)}, u32[]{:S(2)}, u32[]{:S(2)}) collective-permute-start(bf16[224,1024]{1,0:T(8,128)(2,1)} %collective-permute-done.18), channel_id=1, source_target_pairs={{0,2},{1,3},{2,0},{3,1},{4,6},{5,7},{6,4},{7,5},{8,10},{9,11},{10,... | collective-permute-start | bytes 1376264 | tf_op jit(solution)/shard_map/ppermute | solution.py:80
  153.9 19.0 %collective-permute-start.27 = (bf16[256,896]{1,0:T(8,128)(2,1)S(1)}, bf16[256,896]{1,0:T(8,128)(2,1)S(1)}, u32[]{:S(2)}, u32[]{:S(2)}) collective-permute-start(bf16[256,896]{1,0:T(8,128)(2,1)S(1)} %constant_dynamic-slice_fusion.3), channel_id=1, source_target_pairs={{0,16},{1,17},{2,18},{3,19},{4,20},{5,21},{6,22},{7,23},{8,24},{9,... | collective-permute-start | bytes 1376264 | tf_op jit(solution)/shard_map/ppermute | solution.py:80
  205.4 17.7 %collective-permute-start.33 = (bf16[896,384]{1,0:T(8,128)(2,1)S(1)}, bf16[896,384]{1,0:T(8,128)(2,1)S(1)}, u32[]{:S(2)}, u32[]{:S(2)}) collective-permute-start(bf16[896,384]{1,0:T(8,128)(2,1)S(1)} %get-tuple-element.156), channel_id=1, source_target_pairs={{0,16},{1,17},{2,18},{3,19},{4,20},{5,21},{6,22},{7,23},{8,24},{9,... | collective-permute-start | bytes 2064392 | tf_op jit(solution)/shard_map/ppermute | solution.py:80
  211.2 35.7 %collective-permute-start.39 = (bf16[2,4,96,768]{3,2,1,0:T(8,128)(2,1)S(1)}, bf16[2,4,96,768]{3,2,1,0:T(8,128)(2,1)}, u32[]{:S(2)}, u32[]{:S(2)}) collective-permute-start(bf16[2,4,96,768]{3,2,1,0:T(8,128)(2,1)S(1)} %pad_maximum_fusion.11), channel_id=1, source_target_pairs={{0,2},{1,3},{2,0},{3,1},{4,6},{5,7},{6,4},{7,5},{8,10},{9,11},{10,... | collective-permute-start | bytes 3538952 | tf_op jit(solution)/shard_map/ppermute | solution.py:80
  250.9 13.2 %collective-permute-start.41 = (bf16[4,96,768]{2,1,0:T(8,128)(2,1)}, bf16[4,96,768]{2,1,0:T(8,128)(2,1)}, u32[]{:S(2)}, u32[]{:S(2)}) collective-permute-start(bf16[4,96,768]{2,1,0:T(8,128)(2,1)} %pad_maximum_fusion.14), channel_id=1, source_target_pairs={{0,16},{1,17},{2,18},{3,19},{4,20},{5,21},{6,22},{7,23},{8,24},{9,... | collective-permute-start | bytes 1769480 | tf_op jit(solution)/shard_map/ppermute | solution.py:80
  257.6 15.6 %collective-permute-start.40 = (f32[56,384]{1,0:T(8,128)S(1)}, f32[56,384]{1,0:T(8,128)S(1)}, u32[]{:S(2)}, u32[]{:S(2)}) collective-permute-start(f32[56,384]{1,0:T(8,128)S(1)} %get-tuple-element.93), channel_id=1, source_target_pairs={{0,1},{1,0},{2,3},{3,2},{4,5},{5,4},{6,7},{7,6},{8,9},{9,8},{10,11... | collective-permute-start | bytes 258056 | tf_op jit(solution)/shard_map/ppermute | solution.py:80
  (92 other events, 709.4 us)

commit v2 on v1

--- a/solution.py
+++ b/solution.py
@@ -135,7 +135,7 @@
             [("z", "s", 3), ("z", "s", 1), ("y", "s", 0), ("y", "u", 0)],
             [("z", "u", 3), ("z", "s", 2), ("y", "s", 3), ("y", "s", 1), ("x", "s", (0,))],
             [("zz", "u", 1), ("y", "s", 2), ("y", "u", 3), ("x", "s", (1, 3)), ("y", "d", 0)],
-            [("z", "d", 3), ("z", "d", 1), ("y", "u", 1), ("y", "u", 2), ("x", "s", (2,))],
+            [("z", "d", 3), ("z", "d", 1), ("yy", "u", 1), ("x", "s", (2,))],
             [("c", "s", 0), ("z", "d", 2), ("y", "d", 1), ("y", "d", 3)],
             [("y", "d", 2)],
         ]
@@ -149,6 +149,8 @@
     stack, placed = [None], []
 
     def values_of(axis, name, j):
+        if axis == "yy":
+            return held["zz", name, j], MASK_Y
         if axis == "zz":
             return jnp.stack([held["z", name, 0], held["z", name, 3]]), 4
         if axis == "z" and n_z == 4 and j == 2:
@@ -172,6 +174,8 @@
         came = [swap(v, mask) for v, (_, mask) in zip(values, todo)]
         held.update(zip(batch, came))
         for axis, name, j in batch:
+            if axis == "yy":
+                held["y", name, 1], held["y", name, 2] = held[axis, name, j]
             if axis == "zz":
                 held["z", name, 1], held["z", name, 2] = held[axis, name, j]
             if axis == "x":

time: 293 us -> 288 us (0.983)
  waiting for transfers between devices: 105 us -> 110 us
  local copies, waits for them, and re-layouts: 41.6 us -> 37.2 us
    dynamic_update_slice x12, local copies, waits for them, and re-layouts: 11 us -> 5.75 us  [put(): lax.dynamic_update_slice(buffer, values[None], (index,) + (0,) * (buffer....]
    ppermute x44 -> x43, waiting for transfers between devices: 94.9 us -> 99.7 us  [swap(): return lax.ppermute(values, BOTH, [(i, i ^ mask) for i in range(devices)])]
    unnamed x144 -> x154, local copies, waits for them, and re-layouts: 8.87 us -> 12.2 us
    ppermute x44 -> x43, starting transfers between devices: 41.7 us -> 40.5 us  [swap(): return lax.ppermute(values, BOTH, [(i, i ^ mask) for i in range(devices)])]
  transfers between devices with their start and end apart: 46 -> 45, of which waited for: 22 -> 22; matrix products, arithmetic and copies ran while one was open for 36% -> 33% of each run, Pallas kernels for 0% -> 0%
where the time goes in v2:
time: 288 us; the launch traced here: 283 us
  waiting for transfers between devices  110 us (38%)
  starting transfers between devices  47.2 us (16%)
  other arithmetic  42.7 us (15%)
  matrix products  38.3 us (13%)
  local copies, waits for them, and re-layouts  37.2 us (13%)
  between operations  7.28 us (3%)
    ppermute x43, waiting for transfers between devices, swap(): return lax.ppermute(values, BOTH, [(i, i ^ mask) for i in range(devices)])  99.7 us
    ppermute x43, starting transfers between devices, swap(): return lax.ppermute(values, BOTH, [(i, i ^ mask) for i in range(devices)])  40.5 us
    dot_general x28, matrix products, dot(): lax.dot_general(a, b, (((ca,), (cb,)), ((), ())), preferred_element_type=...  37.5 us
    unnamed x154, local copies, waits for them, and re-layouts  12.2 us
    all_to_all x1, waiting for transfers between devices, local(): words = lax.all_to_all(words.reshape(devices, -1, embed), BOTH, 0, 0)  10.7 us
    slice x4, local copies, waits for them, and re-layouts, rows_of(): v[:, begin:begin + size].reshape(half * size, width)  6.44 us
  transfers between devices with their start and end apart: 45, of which 22 were waited for; matrix products, arithmetic and copies ran while one was open for 33% of the time, Pallas kernels for 0%

profile of v2, /device:TPU:0, one launch (start us, length us, event | category | flops | bytes accessed | tf_op | source)
XLA Modules:
  0.0 283.1 jit_solution(7825691624396217395)
XLA Ops:
  10.7 4.7 %collective-permute-start.1 = (bf16[168,768]{1,0:T(8,128)(2,1)}, bf16[168,768]{1,0:T(8,128)(2,1)S(1)}, u32[]{:S(2)}, u32[]{:S(2)}) collective-permute-start(bf16[168,768]{1,0:T(8,128)(2,1)} %pad_maximum_fusion.22), channel_id=1, source_target_pairs={{0,12},{1,13},{2,14},{3,15},{4,8},{5,9},{6,10},{7,11},{8,4},{9,5},... | collective-permute-start | bytes 774152 | tf_op jit(solution)/shard_map/ppermute | solution.py:80
  19.2 5.4 %collective-permute-done.3 = bf16[168,768]{1,0:T(8,128)(2,1)S(1)} collective-permute-done((bf16[168,768]{1,0:T(8,128)(2,1)}, bf16[168,768]{1,0:T(8,128)(2,1)S(1)}, u32[]{:S(2)}, u32[]{:S(2)}) %collective-permute-start.3) | collective-permute-done | bytes 258080 | tf_op jit(solution)/shard_map/ppermute | solution.py:80
  28.7 4.5 %collective-permute-done.4 = bf16[208,1024]{1,0:T(8,128)(2,1)} collective-permute-done((bf16[208,1024]{1,0:T(8,128)(2,1)S(1)}, bf16[208,1024]{1,0:T(8,128)(2,1)}, u32[]{:S(2)}, u32[]{:S(2)}) %collective-permute-start.4) | collective-permute-done | bytes 426016 | tf_op jit(solution)/shard_map/ppermute | solution.py:80
  44.2 4.2 %all-to-all-start = ((f32[32,1,512]{2,1,0:T(1,128)}), f32[32,1,512]{2,1,0:T(1,128)S(1)}, u32[]{:S(2)}, u32[]{:S(2)}) async-start(f32[32,1,512]{2,1,0:T(1,128)} %copy.34), calls=%async_computation | async-start | bytes 131072 | tf_op jit(solution)/shard_map/all_to_all | solution.py:204
  48.6 10.7 %all-to-all-done = f32[32,1,512]{2,1,0:T(1,128)S(1)} async-done(((f32[32,1,512]{2,1,0:T(1,128)}), f32[32,1,512]{2,1,0:T(1,128)S(1)}, u32[]{:S(2)}, u32[]{:S(2)}) %all-to-all-start) | async-done | bytes 65568 | tf_op jit(solution)/shard_map/all_to_all | solution.py:204
  65.5 3.3 %collective-permute-done.13 = bf16[168,768]{1,0:T(8,128)(2,1)S(1)} collective-permute-done((bf16[168,768]{1,0:T(8,128)(2,1)}, bf16[168,768]{1,0:T(8,128)(2,1)S(1)}, u32[]{:S(2)}, u32[]{:S(2)}) %collective-permute-start.13) | collective-permute-done | bytes 258080 | tf_op jit(solution)/shard_map/ppermute | solution.py:80
  73.8 2.8 fusion.5
  76.6 5.7 %collective-permute-done.11 = bf16[2,208,1024]{2,1,0:T(8,128)(2,1)S(1)} collective-permute-done((bf16[2,208,1024]{2,1,0:T(8,128)(2,1)S(1)}, bf16[2,208,1024]{2,1,0:T(8,128)(2,1)S(1)}, u32[]{:S(2)}, u32[]{:S(2)}) %collective-permute-start.11) | collective-permute-done | bytes 852000 | tf_op jit(solution)/shard_map/ppermute | solution.py:80
  85.7 2.8 convolution_convert_fusion
  88.5 3.5 %collective-permute-done.12 = bf16[4,168,768]{2,1,0:T(8,128)(2,1)S(1)} collective-permute-done((bf16[4,168,768]{2,1,0:T(8,128)(2,1)S(1)}, bf16[4,168,768]{2,1,0:T(8,128)(2,1)S(1)}, u32[]{:S(2)}, u32[]{:S(2)}) %collective-permute-start.12) | collective-permute-done | bytes 1032224 | tf_op jit(solution)/shard_map/ppermute | solution.py:80
  97.6 6.6 %collective-permute-done.17 = bf16[2,168,768]{2,1,0:T(8,128)(2,1)S(1)} collective-permute-done((bf16[2,168,768]{2,1,0:T(8,128)(2,1)S(1)}, bf16[2,168,768]{2,1,0:T(8,128)(2,1)S(1)}, u32[]{:S(2)}, u32[]{:S(2)}) %collective-permute-start.17) | collective-permute-done | bytes 516128 | tf_op jit(solution)/shard_map/ppermute | solution.py:80
  107.3 5.5 %collective-permute-done.19 = bf16[224,1024]{1,0:T(8,128)(2,1)S(1)} collective-permute-done((bf16[224,1024]{1,0:T(8,128)(2,1)S(1)}, bf16[224,1024]{1,0:T(8,128)(2,1)S(1)}, u32[]{:S(2)}, u32[]{:S(2)}) %collective-permute-start.19) | collective-permute-done | bytes 458784 | tf_op jit(solution)/shard_map/ppermute | solution.py:80
  123.6 5.1 %fusion.13 = bf16[1024,1024]{1,0:T(8,128)(2,1)S(1)} fusion(bf16[1024,1664]{1,0:T(8,128)(2,1)S(1)} %copy-done.15, bf16[1664,1024]{1,0:T(8,128)(2,1)S(1)} %bitcast.183), kind=kOutput, calls=%fused_computation.18 | convolution fusion | flops 3499098112 | bytes 8912896 | tf_op jit(solution)/shard_map/dot_general | solution.py:29
  128.7 3.8 %collective-permute-done.22 = bf16[224,1024]{1,0:T(8,128)(2,1)S(1)} collective-permute-done((bf16[224,1024]{1,0:T(8,128)(2,1)S(1)}, bf16[224,1024]{1,0:T(8,128)(2,1)S(1)}, u32[]{:S(2)}, u32[]{:S(2)}) %collective-permute-start.22) | collective-permute-done | bytes 458784 | tf_op jit(solution)/shard_map/ppermute | solution.py:80
  147.0 3.4 %add_convert_fusion.1 = bf16[512,896]{1,0:T(8,128)(2,1)S(1)} fusion(bf16[512,896]{1,0:T(8,128)(2,1)} %copy-done.66, bf16[1024,1024]{1,0:T(8,128)(2,1)} %copy-done.72, bf16[224,1024]{1,0:T(8,128)(2,1)} %copy-done.71, bf16[224,1024]{1,0:T(8,128)(2,1)} %copy-done.69, bf16[224,1024]{1,0:T(8,128)(2,1)} %copy-done.67, bf16[224,1024]{1,0:T(8,128)(2,1)} %bitcast.197), kind=kOutput, calls=%fused_computation.41 | convolution fusion | flops 948240384 | bytes 4718592 | tf_op jit(solution)/shard_map/dot_general | solution.py:29
  158.6 7.0 %collective-permute-done.27 = bf16[224,1024]{1,0:T(8,128)(2,1)} collective-permute-done((bf16[224,1024]{1,0:T(8,128)(2,1)}, bf16[224,1024]{1,0:T(8,128)(2,1)}, u32[]{:S(2)}, u32[]{:S(2)}) %collective-permute-start.27) | collective-permute-done | bytes 458784 | tf_op jit(solution)/shard_map/ppermute | solution.py:80
  174.2 11.2 %collective-permute-done.29 = bf16[256,896]{1,0:T(8,128)(2,1)S(1)} collective-permute-done((bf16[256,896]{1,0:T(8,128)(2,1)S(1)}, bf16[256,896]{1,0:T(8,128)(2,1)S(1)}, u32[]{:S(2)}, u32[]{:S(2)}) %collective-permute-start.29) | collective-permute-done | bytes 458784 | tf_op jit(solution)/shard_map/ppermute | solution.py:80
  207.9 10.4 %collective-permute-done.32 = bf16[896,384]{1,0:T(8,128)(2,1)S(1)} collective-permute-done((bf16[896,384]{1,0:T(8,128)(2,1)S(1)}, bf16[896,384]{1,0:T(8,128)(2,1)S(1)}, u32[]{:S(2)}, u32[]{:S(2)}) %collective-permute-start.32) | collective-permute-done | bytes 688160 | tf_op jit(solution)/shard_map/ppermute | solution.py:80
  223.1 8.5 %collective-permute-done.33 = bf16[2,2,2,56,384]{4,3,2,1,0:T(8,128)(2,1)} collective-permute-done((bf16[2,2,2,56,384]{4,3,2,1,0:T(8,128)(2,1)}, bf16[2,2,2,56,384]{4,3,2,1,0:T(8,128)(2,1)}, u32[]{:S(2)}, u32[]{:S(2)}) %collective-permute-start.33) | collective-permute-done | bytes 344096 | tf_op jit(solution)/shard_map/ppermute | solution.py:80
  233.4 3.3 %collective-permute-start.34 = (bf16[2,2,56,384]{3,2,1,0:T(8,128)(2,1)}, bf16[2,2,56,384]{3,2,1,0:T(8,128)(2,1)}, u32[]{:S(2)}, u32[]{:S(2)}) collective-permute-start(bf16[2,2,56,384]{3,2,1,0:T(8,128)(2,1)} %fusion.66), channel_id=1, source_target_pairs={{0,12},{1,13},{2,14},{3,15},{4,8},{5,9},{6,10},{7,11},{8,4},{9,5},... | collective-permute-start | bytes 516104 | tf_op jit(solution)/shard_map/ppermute | solution.py:80
  236.7 4.3 %collective-permute-done.34 = bf16[2,2,56,384]{3,2,1,0:T(8,128)(2,1)} collective-permute-done((bf16[2,2,56,384]{3,2,1,0:T(8,128)(2,1)}, bf16[2,2,56,384]{3,2,1,0:T(8,128)(2,1)}, u32[]{:S(2)}, u32[]{:S(2)}) %collective-permute-start.34) | collective-permute-done | bytes 172064 | tf_op jit(solution)/shard_map/ppermute | solution.py:80
  252.7 6.6 %collective-permute-done.40 = bf16[4,96,768]{2,1,0:T(8,128)(2,1)} collective-permute-done((bf16[4,96,768]{2,1,0:T(8,128)(2,1)}, bf16[4,96,768]{2,1,0:T(8,128)(2,1)}, u32[]{:S(2)}, u32[]{:S(2)}) %collective-permute-start.40) | collective-permute-done | bytes 589856 | tf_op jit(solution)/shard_map/ppermute | solution.py:80
  262.5 4.3 %collective-permute-start.41 = (bf16[2,96,768]{2,1,0:T(8,128)(2,1)S(1)}, bf16[2,96,768]{2,1,0:T(8,128)(2,1)S(1)}, u32[]{:S(2)}, u32[]{:S(2)}) collective-permute-start(bf16[2,96,768]{2,1,0:T(8,128)(2,1)S(1)} %maximum_maximum_fusion), channel_id=1, source_target_pairs={{0,4},{1,5},{2,6},{3,7},{4,0},{5,1},{6,2},{7,3},{8,12},{9,13},{10,... | collective-permute-start | bytes 884744 | tf_op jit(solution)/shard_map/ppermute | solution.py:80
  274.3 5.8 %collective-permute-done.42 = bf16[96,768]{1,0:T(8,128)(2,1)S(1)} collective-permute-done((bf16[96,768]{1,0:T(8,128)(2,1)S(1)}, bf16[96,768]{1,0:T(8,128)(2,1)S(1)}, u32[]{:S(2)}, u32[]{:S(2)}) %collective-permute-start.42) | collective-permute-done | bytes 147488 | tf_op jit(solution)/shard_map/ppermute | solution.py:80
  (360 shorter events, 142.7 us)
Async XLA Ops:
  5.8 64.6 %collective-permute-start.14 = (bf16[512,1664]{1,0:T(8,128)(2,1)}, bf16[512,1664]{1,0:T(8,128)(2,1)}, u32[]{:S(2)}, u32[]{:S(2)}) collective-permute-start(bf16[512,1664]{1,0:T(8,128)(2,1)} %param.13), channel_id=1, source_target_pairs={{0,1},{1,0},{2,3},{3,2},{4,5},{5,4},{6,7},{7,6},{8,9},{9,8},{10,11... | collective-permute-start | bytes 5111816 | tf_op jit(solution)/shard_map/ppermute | solution.py:80
  10.7 22.6 %collective-permute-start.1 = (bf16[168,768]{1,0:T(8,128)(2,1)}, bf16[168,768]{1,0:T(8,128)(2,1)S(1)}, u32[]{:S(2)}, u32[]{:S(2)}) collective-permute-start(bf16[168,768]{1,0:T(8,128)(2,1)} %pad_maximum_fusion.22), channel_id=1, source_target_pairs={{0,12},{1,13},{2,14},{3,15},{4,8},{5,9},{6,10},{7,11},{8,4},{9,5},... | collective-permute-start | bytes 774152 | tf_op jit(solution)/shard_map/ppermute | solution.py:80
  15.4 17.9 %collective-permute-start.2 = (bf16[168,768]{1,0:T(8,128)(2,1)}, bf16[168,768]{1,0:T(8,128)(2,1)S(1)}, u32[]{:S(2)}, u32[]{:S(2)}) collective-permute-start(bf16[168,768]{1,0:T(8,128)(2,1)} %pad_maximum_fusion.22), channel_id=1, source_target_pairs={{0,4},{1,5},{2,6},{3,7},{4,0},{5,1},{6,2},{7,3},{8,12},{9,13},{10,... | collective-permute-start | bytes 774152 | tf_op jit(solution)/shard_map/ppermute | solution.py:80
  16.9 16.3 %collective-permute-start.4 = (bf16[208,1024]{1,0:T(8,128)(2,1)S(1)}, bf16[208,1024]{1,0:T(8,128)(2,1)}, u32[]{:S(2)}, u32[]{:S(2)}) collective-permute-start(bf16[208,1024]{1,0:T(8,128)(2,1)S(1)} %bitcast.179), channel_id=1, source_target_pairs={{0,2},{1,3},{2,0},{3,1},{4,6},{5,7},{6,4},{7,5},{8,10},{9,11},{10,... | collective-permute-start | bytes 1277960 | tf_op jit(solution)/shard_map/ppermute | solution.py:80
  35.1 13.2 %collective-permute-start.7 = (bf16[168,768]{1,0:T(8,128)(2,1)S(1)}, bf16[168,768]{1,0:T(8,128)(2,1)S(1)}, u32[]{:S(2)}, u32[]{:S(2)}) collective-permute-start(bf16[168,768]{1,0:T(8,128)(2,1)S(1)} %collective-permute-done.2), channel_id=1, source_target_pairs={{0,2},{1,3},{2,0},{3,1},{4,6},{5,7},{6,4},{7,5},{8,10},{9,11},{10,... | collective-permute-start | bytes 774152 | tf_op jit(solution)/shard_map/ppermute | solution.py:80
  37.1 22.2 %collective-permute-start.5 = (bf16[208,1024]{1,0:T(8,128)(2,1)S(1)}, bf16[208,1024]{1,0:T(8,128)(2,1)S(1)}, u32[]{:S(2)}, u32[]{:S(2)}) collective-permute-start(bf16[208,1024]{1,0:T(8,128)(2,1)S(1)} %bitcast.180), channel_id=1, source_target_pairs={{0,12},{1,13},{2,14},{3,15},{4,8},{5,9},{6,10},{7,11},{8,4},{9,5},... | collective-permute-start | bytes 1277960 | tf_op jit(solution)/shard_map/ppermute | solution.py:80
  42.0 17.4 %collective-permute-start.10 = (bf16[2,168,768]{2,1,0:T(8,128)(2,1)}, bf16[2,168,768]{2,1,0:T(8,128)(2,1)}, u32[]{:S(2)}, u32[]{:S(2)}) collective-permute-start(bf16[2,168,768]{2,1,0:T(8,128)(2,1)} %pad_maximum_fusion.15), channel_id=1, source_target_pairs={{0,16},{1,17},{2,18},{3,19},{4,20},{5,21},{6,22},{7,23},{8,24},{9,... | collective-permute-start | bytes 1548296 | tf_op jit(solution)/shard_map/ppermute | solution.py:80
  44.2 15.1 %all-to-all-start = ((f32[32,1,512]{2,1,0:T(1,128)}), f32[32,1,512]{2,1,0:T(1,128)S(1)}, u32[]{:S(2)}, u32[]{:S(2)}) async-start(f32[32,1,512]{2,1,0:T(1,128)} %copy.34), calls=%async_computation | async-start | bytes 131072 | tf_op jit(solution)/shard_map/all_to_all | solution.py:204
  60.4 28.1 %collective-permute-start.15 = (bf16[208,1024]{1,0:T(8,128)(2,1)S(1)}, bf16[208,1024]{1,0:T(8,128)(2,1)S(1)}, u32[]{:S(2)}, u32[]{:S(2)}) collective-permute-start(bf16[208,1024]{1,0:T(8,128)(2,1)S(1)} %collective-permute-done.5), channel_id=1, source_target_pairs={{0,2},{1,3},{2,0},{3,1},{4,6},{5,7},{6,4},{7,5},{8,10},{9,11},{10,... | collective-permute-start | bytes 1277960 | tf_op jit(solution)/shard_map/ppermute | solution.py:80
  61.6 27.0 %collective-permute-start.16 = (bf16[224,1024]{1,0:T(8,128)(2,1)}, bf16[224,1024]{1,0:T(8,128)(2,1)S(1)}, u32[]{:S(2)}, u32[]{:S(2)}) collective-permute-start(bf16[224,1024]{1,0:T(8,128)(2,1)} %bitcast.196), channel_id=1, source_target_pairs={{0,2},{1,3},{2,0},{3,1},{4,6},{5,7},{6,4},{7,5},{8,10},{9,11},{10,... | collective-permute-start | bytes 1376264 | tf_op jit(solution)/shard_map/ppermute | solution.py:80
  62.4 19.9 %collective-permute-start.11 = (bf16[2,208,1024]{2,1,0:T(8,128)(2,1)S(1)}, bf16[2,208,1024]{2,1,0:T(8,128)(2,1)S(1)}, u32[]{:S(2)}, u32[]{:S(2)}) collective-permute-start(bf16[2,208,1024]{2,1,0:T(8,128)(2,1)S(1)} %pad_maximum_fusion.13), channel_id=1, source_target_pairs={{0,4},{1,5},{2,6},{3,7},{4,0},{5,1},{6,2},{7,3},{8,12},{9,13},{10,... | collective-permute-start | bytes 2555912 | tf_op jit(solution)/shard_map/ppermute | solution.py:80
  68.8 23.2 %collective-permute-start.12 = (bf16[4,168,768]{2,1,0:T(8,128)(2,1)S(1)}, bf16[4,168,768]{2,1,0:T(8,128)(2,1)S(1)}, u32[]{:S(2)}, u32[]{:S(2)}) collective-permute-start(bf16[4,168,768]{2,1,0:T(8,128)(2,1)S(1)} %pad_maximum_fusion.12), channel_id=1, source_target_pairs={{0,16},{1,17},{2,18},{3,19},{4,20},{5,21},{6,22},{7,23},{8,24},{9,... | collective-permute-start | bytes 3096584 | tf_op jit(solution)/shard_map/ppermute | solution.py:80
  92.0 15.3 %collective-permute-start.18 = (bf16[224,1024]{1,0:T(8,128)(2,1)S(1)}, bf16[224,1024]{1,0:T(8,128)(2,1)S(1)}, u32[]{:S(2)}, u32[]{:S(2)}) collective-permute-start(bf16[224,1024]{1,0:T(8,128)(2,1)S(1)} %bitcast.198), channel_id=1, source_target_pairs={{0,12},{1,13},{2,14},{3,15},{4,8},{5,9},{6,10},{7,11},{8,4},{9,5},... | collective-permute-start | bytes 1376264 | tf_op jit(solution)/shard_map/ppermute | solution.py:80
  93.3 19.5 %collective-permute-start.19 = (bf16[224,1024]{1,0:T(8,128)(2,1)S(1)}, bf16[224,1024]{1,0:T(8,128)(2,1)S(1)}, u32[]{:S(2)}, u32[]{:S(2)}) collective-permute-start(bf16[224,1024]{1,0:T(8,128)(2,1)S(1)} %bitcast.199), channel_id=1, source_target_pairs={{0,4},{1,5},{2,6},{3,7},{4,0},{5,1},{6,2},{7,3},{8,12},{9,13},{10,... | collective-permute-start | bytes 1376264 | tf_op jit(solution)/shard_map/ppermute | solution.py:80
  93.8 19.0 %collective-permute-start.20 = (bf16[2,208,1024]{2,1,0:T(8,128)(2,1)S(1)}, bf16[2,208,1024]{2,1,0:T(8,128)(2,1)S(1)}, u32[]{:S(2)}, u32[]{:S(2)}) collective-permute-start(bf16[2,208,1024]{2,1,0:T(8,128)(2,1)S(1)} %collective-permute-done.11), channel_id=1, source_target_pairs={{0,2},{1,3},{2,0},{3,1},{4,6},{5,7},{6,4},{7,5},{8,10},{9,11},{10,... | collective-permute-start | bytes 2555912 | tf_op jit(solution)/shard_map/ppermute | solution.py:80
  113.5 22.2 %collective-permute-start.21 = (bf16[16,168,768]{2,1,0:T(8,128)(2,1)}, bf16[16,168,768]{2,1,0:T(8,128)(2,1)}, u32[]{:S(2)}, u32[]{:S(2)}) collective-permute-start(bf16[16,168,768]{2,1,0:T(8,128)(2,1)} %bitcast.28), channel_id=1, source_target_pairs={{0,1},{1,0},{2,3},{3,2},{4,5},{5,4},{6,7},{7,6},{8,9},{9,8},{10,11... | collective-permute-start | bytes 12386312 | tf_op jit(solution)/shard_map/ppermute | solution.py:80
  119.1 13.4 %collective-permute-start.22 = (bf16[224,1024]{1,0:T(8,128)(2,1)S(1)}, bf16[224,1024]{1,0:T(8,128)(2,1)S(1)}, u32[]{:S(2)}, u32[]{:S(2)}) collective-permute-start(bf16[224,1024]{1,0:T(8,128)(2,1)S(1)} %copy-done.70), channel_id=1, source_target_pairs={{0,2},{1,3},{2,0},{3,1},{4,6},{5,7},{6,4},{7,5},{8,10},{9,11},{10,... | collective-permute-start | bytes 1376264 | tf_op jit(solution)/shard_map/ppermute | solution.py:80
  119.4 14.5 %collective-permute-start.23 = (bf16[224,1024]{1,0:T(8,128)(2,1)S(1)}, bf16[224,1024]{1,0:T(8,128)(2,1)}, u32[]{:S(2)}, u32[]{:S(2)}) collective-permute-start(bf16[224,1024]{1,0:T(8,128)(2,1)S(1)} %copy-done.47), channel_id=1, source_target_pairs={{0,4},{1,5},{2,6},{3,7},{4,0},{5,1},{6,2},{7,3},{8,12},{9,13},{10,... | collective-permute-start | bytes 1376264 | tf_op jit(solution)/shard_map/ppermute | solution.py:80
  119.8 22.1 %collective-permute-start.25 = (bf16[224,1024]{1,0:T(8,128)(2,1)S(1)}, bf16[224,1024]{1,0:T(8,128)(2,1)S(1)}, u32[]{:S(2)}, u32[]{:S(2)}) collective-permute-start(bf16[224,1024]{1,0:T(8,128)(2,1)S(1)} %copy-done.47), channel_id=1, source_target_pairs={{0,2},{1,3},{2,0},{3,1},{4,6},{5,7},{6,4},{7,5},{8,10},{9,11},{10,... | collective-permute-start | bytes 1376264 | tf_op jit(solution)/shard_map/ppermute | solution.py:80
  151.3 16.9 %collective-permute-start.26 = (bf16[256,896]{1,0:T(8,128)(2,1)}, bf16[256,896]{1,0:T(8,128)(2,1)S(1)}, u32[]{:S(2)}, u32[]{:S(2)}) collective-permute-start(bf16[256,896]{1,0:T(8,128)(2,1)} %constant_dynamic-slice_fusion.3), channel_id=1, source_target_pairs={{0,16},{1,17},{2,18},{3,19},{4,20},{5,21},{6,22},{7,23},{8,24},{9,... | collective-permute-start | bytes 1376264 | tf_op jit(solution)/shard_map/ppermute | solution.py:80
  200.6 17.7 %collective-permute-start.32 = (bf16[896,384]{1,0:T(8,128)(2,1)S(1)}, bf16[896,384]{1,0:T(8,128)(2,1)S(1)}, u32[]{:S(2)}, u32[]{:S(2)}) collective-permute-start(bf16[896,384]{1,0:T(8,128)(2,1)S(1)} %get-tuple-element.151), channel_id=1, source_target_pairs={{0,16},{1,17},{2,18},{3,19},{4,20},{5,21},{6,22},{7,23},{8,24},{9,... | collective-permute-start | bytes 2064392 | tf_op jit(solution)/shard_map/ppermute | solution.py:80
  206.4 35.8 %collective-permute-start.38 = (bf16[2,4,96,768]{3,2,1,0:T(8,128)(2,1)S(1)}, bf16[2,4,96,768]{3,2,1,0:T(8,128)(2,1)}, u32[]{:S(2)}, u32[]{:S(2)}) collective-permute-start(bf16[2,4,96,768]{3,2,1,0:T(8,128)(2,1)S(1)} %pad_maximum_fusion.11), channel_id=1, source_target_pairs={{0,2},{1,3},{2,0},{3,1},{4,6},{5,7},{6,4},{7,5},{8,10},{9,11},{10,... | collective-permute-start | bytes 3538952 | tf_op jit(solution)/shard_map/ppermute | solution.py:80
  246.1 13.2 %collective-permute-start.40 = (bf16[4,96,768]{2,1,0:T(8,128)(2,1)}, bf16[4,96,768]{2,1,0:T(8,128)(2,1)}, u32[]{:S(2)}, u32[]{:S(2)}) collective-permute-start(bf16[4,96,768]{2,1,0:T(8,128)(2,1)} %pad_maximum_fusion.14), channel_id=1, source_target_pairs={{0,16},{1,17},{2,18},{3,19},{4,20},{5,21},{6,22},{7,23},{8,24},{9,... | collective-permute-start | bytes 1769480 | tf_op jit(solution)/shard_map/ppermute | solution.py:80
  252.7 16.0 %collective-permute-start.39 = (f32[56,384]{1,0:T(8,128)S(1)}, f32[56,384]{1,0:T(8,128)S(1)}, u32[]{:S(2)}, u32[]{:S(2)}) collective-permute-start(f32[56,384]{1,0:T(8,128)S(1)} %get-tuple-element.91), channel_id=1, source_target_pairs={{0,1},{1,0},{2,3},{3,2},{4,5},{5,4},{6,7},{7,6},{8,9},{9,8},{10,11... | collective-permute-start | bytes 258056 | tf_op jit(solution)/shard_map/ppermute | solution.py:80
  (96 other events, 707.6 us)
